TPU v7x, 256 devices: a whole 4x4x8 slice. The times are simulated.
256 devices in a mesh: ctx: 64 (over x, z, core), head: 4 (over y).
Axes of the slice: x: 4, y: 4, z: 8, core: 2. Of those that a mesh axis runs over, the one named last changes fastest.
Arguments:
- queries: bfloat16 [16384, 2048], P('ctx', 'head'), may hold values from -160 to 160
- keys: bfloat16 [16384, 512], P('ctx', 'head'), may hold values from -7 to 7
- values: bfloat16 [16384, 512], P('ctx', 'head'), may hold values from -6 to 6
- segments: int32 [16384], P('ctx'), may hold values from 0 to 2, as said below
- block_ranges: int32 [128, 3], replicated, may hold values from 0 to 127, as said below
- owner: int32 [128], replicated, may hold values from 0 to 63, as said below
- out_proj: bfloat16 [2048, 4096], P('head'), may hold values from -0.125 to 0.125
Outputs:
- attended: bfloat16 [16384, 4096], P(('ctx', 'head'))
Inputs may be any that keep to these rules, and one draw needn't show every extreme that they name: `owner`: each index d of ctx owns exactly one block b with b % 2 == j for every j below 2. `block_ranges`: row b holds lo <= b <= hi and a flag of 0 or 1; hi == b where the flag is 1. `segments`: never falling along the tokens; 3 documents.
All inputs are finite; a program needn't handle non-finite values.
Results may differ from a plain program's by a relative error of at most 0.015.
Values may be sent and summed in bfloat16 or wider, within the bound.
A program may use at most 128 MiB of HBM per device.

v0:
```python
import math

import jax
import jax.numpy as jnp
from jax import lax
from jax.sharding import PartitionSpec as P

HD = 128
QH = 16
KH = 4
BLK = 128


masked_score = -1e30


def local(queries, keys, values, segments, block_ranges, owner, out_proj):
    ctx_index = lax.axis_index("ctx")
    row_count = queries.shape[0]
    block_count = row_count // BLK
    kv_local = keys.shape[1] // HD
    group_size = QH // KH
    heads_local = kv_local * group_size
    score_scale = 1.0 / math.sqrt(HD)
    local_ids = jnp.arange(block_count, dtype=jnp.int32)
    query_blocks = queries.reshape(block_count, BLK, heads_local * HD)
    seg_blocks = segments.reshape(block_count, BLK)
    every_block = jnp.arange(owner.shape[0], dtype=jnp.int32)
    matches = (owner[None, :] == ctx_index) & (
        every_block[None, :] % block_count == local_ids[:, None]
    )
    wanted = jnp.sum(jnp.where(matches, every_block[None, :], 0), axis=1)
    shard_piece = (
        lax.all_gather(query_blocks, "ctx", axis=0, tiled=True),
        lax.all_gather(seg_blocks, "ctx", axis=0, tiled=True),
    )
    piece_len = shard_piece[0].shape[0]
    offset = wanted
    inside = (offset >= 0) & (offset < piece_len)
    place = jnp.clip(offset, 0, piece_len - 1)
    taken_query = jnp.take(shard_piece[0], place, axis=0)
    taken_seg = jnp.take(shard_piece[1], place, axis=0)
    own_query = jnp.where(inside[:, None, None], taken_query, jnp.zeros_like(query_blocks))
    own_seg = jnp.where(inside[:, None], taken_seg, jnp.zeros_like(seg_blocks))
    ranges_own = jnp.take(block_ranges, wanted, axis=0)
    low_blocks = ranges_own[:, 0]
    high_blocks = ranges_own[:, 1]
    low_rows = jnp.repeat(low_blocks, BLK, total_repeat_length=row_count)
    high_rows = jnp.repeat(high_blocks, BLK, total_repeat_length=row_count)
    causal_rows = jnp.repeat(ranges_own[:, 2], BLK, total_repeat_length=row_count)
    pos_rows = (wanted[:, None] * BLK + jnp.arange(BLK, dtype=jnp.int32)[None, :]).reshape(
        row_count
    )
    seg_rows = own_seg.reshape(row_count)
    query_heads = own_query.reshape(row_count, kv_local, group_size, HD)
    start_state = (
        jnp.full((kv_local, group_size, row_count), masked_score, jnp.float32),
        jnp.zeros((kv_local, group_size, row_count), jnp.float32),
        jnp.zeros((kv_local, group_size, row_count, HD), jnp.float32),
    )
    key_piece = lax.all_gather(keys, "ctx", axis=0, tiled=True)
    value_piece = lax.all_gather(values, "ctx", axis=0, tiled=True)
    seg_piece = lax.all_gather(segments, "ctx", axis=0, tiled=True)
    piece_len = key_piece.shape[0]
    width = math.gcd(piece_len, 1024)

    def one_step(step_index, current):
        offset = step_index * width
        key_step = lax.dynamic_slice_in_dim(key_piece, offset, width, 0).reshape(
            width, kv_local, HD
        )
        value_step = lax.dynamic_slice_in_dim(value_piece, offset, width, 0).reshape(
            width, kv_local, HD
        )
        seg_step = lax.dynamic_slice_in_dim(seg_piece, offset, width, 0)
        key_pos = offset + jnp.arange(width, dtype=jnp.int32)
        key_block = key_pos // BLK
        touches = jnp.any(
            (low_blocks <= (offset + width - 1) // BLK) & (high_blocks >= offset // BLK)
        )

        def update(inner):
            largest, denom, numer = inner
            visible = (key_block[None, :] >= low_rows[:, None]) & (
                key_block[None, :] <= high_rows[:, None]
            )
            visible = visible & (seg_rows[:, None] == seg_step[None, :])
            visible = visible & (
                (causal_rows[:, None] == 0) | (key_pos[None, :] <= pos_rows[:, None])
            )
            score = (
                jnp.einsum(
                    "rgcd,kgd->gcrk", query_heads, key_step, preferred_element_type=jnp.float32
                )
                * score_scale
            )
            score = jnp.where(visible, score, masked_score)
            new_largest = jnp.maximum(largest, jnp.max(score, axis=-1))
            expo = jnp.where(visible, jnp.exp(score - new_largest[..., None]), 0.0)
            factor = jnp.exp(largest - new_largest)
            new_denom = denom * factor + jnp.sum(expo, axis=-1)
            new_numer = numer * factor[..., None] + jnp.einsum(
                "gcrk,kgd->gcrd",
                expo.astype(jnp.bfloat16),
                value_step,
                preferred_element_type=jnp.float32,
            )
            return (new_largest, new_denom, new_numer)

        return lax.cond(touches, update, lambda inner: inner, current)

    largest, denom, numer = lax.fori_loop(0, piece_len // width, one_step, start_state)
    attn = (
        (numer / denom[..., None])
        .transpose(2, 0, 1, 3)
        .reshape(row_count, heads_local * HD)
        .astype(jnp.bfloat16)
    )
    return lax.psum_scatter(
        jnp.dot(attn, out_proj, preferred_element_type=jnp.float32).astype(jnp.bfloat16),
        "head",
        scatter_dimension=0,
        tiled=True,
    )


def solution(mesh):
    return jax.shard_map(
        local,
        mesh=mesh,
        in_specs=(
            P("ctx", "head"),
            P("ctx", "head"),
            P("ctx", "head"),
            P("ctx"),
            P(),
            P(),
            P("head", None),
        ),
        out_specs=P(("ctx", "head"), None),
        check_vma=False,
    )
```

profile of v0, /device:TPU:1, one launch (start us, length us, event | category | flops | bytes accessed | tf_op | source)
XLA Modules:
  0.0 434.1 jit_solution(16893205177072106195)
XLA Ops:
  10.9 48.2 %all-gather = s32[64,2,128]{2,1,0:T(2,128)S(1)} all-gather(s32[1,2,128]{2,1,0:T(2,128)} %bitcast.110), channel_id=1, replica_groups=mesh['ctx'=64,'head'=4] {'ctx'}, dimensions={0}, use_global_device_ids=true | all-gather | bytes 66560 | tf_op jit(solution)/shard_map/all_gather | solution.py:35
  59.7 42.7 %all-gather.1 = s32[64,1,256]{2,1,0:T(1,128)S(1)} all-gather(s32[1,1,256]{2,1,0:T(1,128)} %bitcast.111), channel_id=1, replica_groups=mesh['ctx'=64,'head'=4] {'ctx'}, dimensions={0}, use_global_device_ids=true | all-gather | bytes 66560 | tf_op jit(solution)/shard_map/all_gather | solution.py:63
  103.4 1.2 select_select_fusion.1
  104.6 1.2 select_select_fusion.2
  106.4 1.2 select_select_fusion.3
  107.8 6.5 %all-gather.8.cloned.1.call-done = bf16[128,128,512]{2,1,0:T(8,128)(2,1)} async-done(((bf16[2,128,512]{2,1,0:T(8,128)(2,1)}), bf16[128,128,512]{2,1,0:T(8,128)(2,1)}) %all-gather.8.cloned.1.call-update) | async-done | bytes 16777232 | tf_op jit(solution)/shard_map/all_gather | solution.py:34
  114.3 6.3 %gather_fusion.2 = bf16[2,128,512]{2,1,0:T(8,128)(2,1)S(1)} fusion(bf16[128,128,512]{2,1,0:T(8,128)(2,1)} %all-gather.8.cloned.1.call-done, s32[1024]{0:T(1024)S(1)} %pad_clamp_fusion), kind=kCustom, calls=%fused_computation.2 | custom fusion | bytes 524296 | tf_op jit(solution)/shard_map/jit(_take)/gather | solution.py:41
  120.7 1.3 select_select_fusion
  122.0 71.1 %all-gather.10.cloned.1.call-done = bf16[16384,128]{1,0:T(8,128)(2,1)} async-done(((bf16[256,128]{1,0:T(8,128)(2,1)}), bf16[16384,128]{1,0:T(8,128)(2,1)}) %all-gather.10.cloned.1.call-update) | async-done | bytes 4194320 | tf_op jit(solution)/shard_map/all_gather | solution.py:62
  193.1 79.1 %all-gather.6.cloned.1.call-done = bf16[16384,128]{1,0:T(8,128)(2,1)} async-done(((bf16[256,128]{1,0:T(8,128)(2,1)}), bf16[16384,128]{1,0:T(8,128)(2,1)}) %all-gather.6.cloned.1.call-update) | async-done | bytes 4194320 | tf_op jit(solution)/shard_map/all_gather | solution.py:61
  272.3 120.9 %while.26 = (s32[]{:T(128)}, f32[1,4,256]{2,1,0:T(4,128)S(1)}, f32[1,4,256]{2,1,0:T(4,128)S(1)}, f32[1,4,256,128]{3,2,1,0:T(8,128)S(1)}, s32[2]{0:T(128)S(1)}, /...) while((s32[]{:T(128)}, f32[1,4,256]{2,1,0:T(4,128)S(1)}, ...), condition=%wide.region_7.9_spmd.clone, body=%wide.region_1.8_spmd.clone.sunk | while | flops 552881728 | bytes 15578404 | solution.py:112
  273.6 6.2 %conditional.3 = ((f32[1,4,256]{2,1,0:T(4,128)S(1)}, f32[1,4,256]{2,1,0:T(4,128)S(1)}, f32[1,4,256,128]{3,2,1,0:T(8,128)S(1)})) conditional(s32[]{:T(128)} %convert_element_type.50, (f32[1,4,256]{2,1,0:T(4,128)S(1)}, f32[1,4,256]{2,1,0:T(4,128)S(1)}, f32[1,4,256,128]{3,2,1,0:T(8,128)S(1)}) %tuple.106, (s32[]{:T(128)}, s32[1024]{0:T(1024)S(1)}, ...), branch_computations={%region_3.4_spmd, %region_4.7_spmd.clone} | conditional | flops 552881664 | bytes 15572565 | solution.py:110
  274.5 1.8 fusion.2
  276.3 2.4 fusion.12
  278.8 1.0 fusion.4
  281.2 6.2 %conditional.3 = ((f32[1,4,256]{2,1,0:T(4,128)S(1)}, f32[1,4,256]{2,1,0:T(4,128)S(1)}, f32[1,4,256,128]{3,2,1,0:T(8,128)S(1)})) conditional(s32[]{:T(128)} %convert_element_type.50, (f32[1,4,256]{2,1,0:T(4,128)S(1)}, f32[1,4,256]{2,1,0:T(4,128)S(1)}, f32[1,4,256,128]{3,2,1,0:T(8,128)S(1)}) %tuple.106, (s32[]{:T(128)}, s32[1024]{0:T(1024)S(1)}, ...), branch_computations={%region_3.4_spmd, %region_4.7_spmd.clone} | conditional | flops 552881664 | bytes 15572565 | solution.py:110
  282.1 1.8 fusion.2
  283.9 2.4 fusion.12
  288.7 6.2 %conditional.3 = ((f32[1,4,256]{2,1,0:T(4,128)S(1)}, f32[1,4,256]{2,1,0:T(4,128)S(1)}, f32[1,4,256,128]{3,2,1,0:T(8,128)S(1)})) conditional(s32[]{:T(128)} %convert_element_type.50, (f32[1,4,256]{2,1,0:T(4,128)S(1)}, f32[1,4,256]{2,1,0:T(4,128)S(1)}, f32[1,4,256,128]{3,2,1,0:T(8,128)S(1)}) %tuple.106, (s32[]{:T(128)}, s32[1024]{0:T(1024)S(1)}, ...), branch_computations={%region_3.4_spmd, %region_4.7_spmd.clone} | conditional | flops 552881664 | bytes 15572565 | solution.py:110
  289.7 1.8 fusion.2
  291.4 2.4 fusion.12
  296.3 6.2 %conditional.3 = ((f32[1,4,256]{2,1,0:T(4,128)S(1)}, f32[1,4,256]{2,1,0:T(4,128)S(1)}, f32[1,4,256,128]{3,2,1,0:T(8,128)S(1)})) conditional(s32[]{:T(128)} %convert_element_type.50, (f32[1,4,256]{2,1,0:T(4,128)S(1)}, f32[1,4,256]{2,1,0:T(4,128)S(1)}, f32[1,4,256,128]{3,2,1,0:T(8,128)S(1)}) %tuple.106, (s32[]{:T(128)}, s32[1024]{0:T(1024)S(1)}, ...), branch_computations={%region_3.4_spmd, %region_4.7_spmd.clone} | conditional | flops 552881664 | bytes 15572565 | solution.py:110
  297.2 1.8 fusion.2
  299.0 2.4 fusion.12
  303.8 6.2 %conditional.3 = ((f32[1,4,256]{2,1,0:T(4,128)S(1)}, f32[1,4,256]{2,1,0:T(4,128)S(1)}, f32[1,4,256,128]{3,2,1,0:T(8,128)S(1)})) conditional(s32[]{:T(128)} %convert_element_type.50, (f32[1,4,256]{2,1,0:T(4,128)S(1)}, f32[1,4,256]{2,1,0:T(4,128)S(1)}, f32[1,4,256,128]{3,2,1,0:T(8,128)S(1)}) %tuple.106, (s32[]{:T(128)}, s32[1024]{0:T(1024)S(1)}, ...), branch_computations={%region_3.4_spmd, %region_4.7_spmd.clone} | conditional | flops 552881664 | bytes 15572565 | solution.py:110
  304.8 1.8 fusion.2
  306.5 2.4 fusion.12
  309.0 1.0 fusion.4
  311.4 6.2 %conditional.3 = ((f32[1,4,256]{2,1,0:T(4,128)S(1)}, f32[1,4,256]{2,1,0:T(4,128)S(1)}, f32[1,4,256,128]{3,2,1,0:T(8,128)S(1)})) conditional(s32[]{:T(128)} %convert_element_type.50, (f32[1,4,256]{2,1,0:T(4,128)S(1)}, f32[1,4,256]{2,1,0:T(4,128)S(1)}, f32[1,4,256,128]{3,2,1,0:T(8,128)S(1)}) %tuple.106, (s32[]{:T(128)}, s32[1024]{0:T(1024)S(1)}, ...), branch_computations={%region_3.4_spmd, %region_4.7_spmd.clone} | conditional | flops 552881664 | bytes 15572565 | solution.py:110
  312.3 1.8 fusion.2
  314.1 2.4 fusion.12
  319.0 6.2 %conditional.3 = ((f32[1,4,256]{2,1,0:T(4,128)S(1)}, f32[1,4,256]{2,1,0:T(4,128)S(1)}, f32[1,4,256,128]{3,2,1,0:T(8,128)S(1)})) conditional(s32[]{:T(128)} %convert_element_type.50, (f32[1,4,256]{2,1,0:T(4,128)S(1)}, f32[1,4,256]{2,1,0:T(4,128)S(1)}, f32[1,4,256,128]{3,2,1,0:T(8,128)S(1)}) %tuple.106, (s32[]{:T(128)}, s32[1024]{0:T(1024)S(1)}, ...), branch_computations={%region_3.4_spmd, %region_4.7_spmd.clone} | conditional | flops 552881664 | bytes 15572565 | solution.py:110
  319.9 1.8 fusion.2
  321.7 2.4 fusion.12
  326.5 6.2 %conditional.3 = ((f32[1,4,256]{2,1,0:T(4,128)S(1)}, f32[1,4,256]{2,1,0:T(4,128)S(1)}, f32[1,4,256,128]{3,2,1,0:T(8,128)S(1)})) conditional(s32[]{:T(128)} %convert_element_type.50, (f32[1,4,256]{2,1,0:T(4,128)S(1)}, f32[1,4,256]{2,1,0:T(4,128)S(1)}, f32[1,4,256,128]{3,2,1,0:T(8,128)S(1)}) %tuple.106, (s32[]{:T(128)}, s32[1024]{0:T(1024)S(1)}, ...), branch_computations={%region_3.4_spmd, %region_4.7_spmd.clone} | conditional | flops 552881664 | bytes 15572565 | solution.py:110
  327.4 1.8 fusion.2
  329.2 2.4 fusion.12
  334.1 6.2 %conditional.3 = ((f32[1,4,256]{2,1,0:T(4,128)S(1)}, f32[1,4,256]{2,1,0:T(4,128)S(1)}, f32[1,4,256,128]{3,2,1,0:T(8,128)S(1)})) conditional(s32[]{:T(128)} %convert_element_type.50, (f32[1,4,256]{2,1,0:T(4,128)S(1)}, f32[1,4,256]{2,1,0:T(4,128)S(1)}, f32[1,4,256,128]{3,2,1,0:T(8,128)S(1)}) %tuple.106, (s32[]{:T(128)}, s32[1024]{0:T(1024)S(1)}, ...), branch_computations={%region_3.4_spmd, %region_4.7_spmd.clone} | conditional | flops 552881664 | bytes 15572565 | solution.py:110
  335.0 1.8 fusion.2
  336.8 2.4 fusion.12
  341.6 6.2 %conditional.3 = ((f32[1,4,256]{2,1,0:T(4,128)S(1)}, f32[1,4,256]{2,1,0:T(4,128)S(1)}, f32[1,4,256,128]{3,2,1,0:T(8,128)S(1)})) conditional(s32[]{:T(128)} %convert_element_type.50, (f32[1,4,256]{2,1,0:T(4,128)S(1)}, f32[1,4,256]{2,1,0:T(4,128)S(1)}, f32[1,4,256,128]{3,2,1,0:T(8,128)S(1)}) %tuple.106, (s32[]{:T(128)}, s32[1024]{0:T(1024)S(1)}, ...), branch_computations={%region_3.4_spmd, %region_4.7_spmd.clone} | conditional | flops 552881664 | bytes 15572565 | solution.py:110
  342.5 1.8 fusion.2
  344.3 2.4 fusion.12
  349.2 6.2 %conditional.3 = ((f32[1,4,256]{2,1,0:T(4,128)S(1)}, f32[1,4,256]{2,1,0:T(4,128)S(1)}, f32[1,4,256,128]{3,2,1,0:T(8,128)S(1)})) conditional(s32[]{:T(128)} %convert_element_type.50, (f32[1,4,256]{2,1,0:T(4,128)S(1)}, f32[1,4,256]{2,1,0:T(4,128)S(1)}, f32[1,4,256,128]{3,2,1,0:T(8,128)S(1)}) %tuple.106, (s32[]{:T(128)}, s32[1024]{0:T(1024)S(1)}, ...), branch_computations={%region_3.4_spmd, %region_4.7_spmd.clone} | conditional | flops 552881664 | bytes 15572565 | solution.py:110
  350.1 1.8 fusion.2
  351.9 2.4 fusion.12
  356.7 6.2 %conditional.3 = ((f32[1,4,256]{2,1,0:T(4,128)S(1)}, f32[1,4,256]{2,1,0:T(4,128)S(1)}, f32[1,4,256,128]{3,2,1,0:T(8,128)S(1)})) conditional(s32[]{:T(128)} %convert_element_type.50, (f32[1,4,256]{2,1,0:T(4,128)S(1)}, f32[1,4,256]{2,1,0:T(4,128)S(1)}, f32[1,4,256,128]{3,2,1,0:T(8,128)S(1)}) %tuple.106, (s32[]{:T(128)}, s32[1024]{0:T(1024)S(1)}, ...), branch_computations={%region_3.4_spmd, %region_4.7_spmd.clone} | conditional | flops 552881664 | bytes 15572565 | solution.py:110
  357.6 1.8 fusion.2
  359.4 2.4 fusion.12
  364.3 6.2 %conditional.3 = ((f32[1,4,256]{2,1,0:T(4,128)S(1)}, f32[1,4,256]{2,1,0:T(4,128)S(1)}, f32[1,4,256,128]{3,2,1,0:T(8,128)S(1)})) conditional(s32[]{:T(128)} %convert_element_type.50, (f32[1,4,256]{2,1,0:T(4,128)S(1)}, f32[1,4,256]{2,1,0:T(4,128)S(1)}, f32[1,4,256,128]{3,2,1,0:T(8,128)S(1)}) %tuple.106, (s32[]{:T(128)}, s32[1024]{0:T(1024)S(1)}, ...), branch_computations={%region_3.4_spmd, %region_4.7_spmd.clone} | conditional | flops 552881664 | bytes 15572565 | solution.py:110
  365.2 1.8 fusion.2
  367.0 2.4 fusion.12
  371.8 6.2 %conditional.3 = ((f32[1,4,256]{2,1,0:T(4,128)S(1)}, f32[1,4,256]{2,1,0:T(4,128)S(1)}, f32[1,4,256,128]{3,2,1,0:T(8,128)S(1)})) conditional(s32[]{:T(128)} %convert_element_type.50, (f32[1,4,256]{2,1,0:T(4,128)S(1)}, f32[1,4,256]{2,1,0:T(4,128)S(1)}, f32[1,4,256,128]{3,2,1,0:T(8,128)S(1)}) %tuple.106, (s32[]{:T(128)}, s32[1024]{0:T(1024)S(1)}, ...), branch_computations={%region_3.4_spmd, %region_4.7_spmd.clone} | conditional | flops 552881664 | bytes 15572565 | solution.py:110
  372.7 1.8 fusion.2
  374.5 2.4 fusion.12
  377.0 1.0 fusion.4
  379.4 6.2 %conditional.3 = ((f32[1,4,256]{2,1,0:T(4,128)S(1)}, f32[1,4,256]{2,1,0:T(4,128)S(1)}, f32[1,4,256,128]{3,2,1,0:T(8,128)S(1)})) conditional(s32[]{:T(128)} %convert_element_type.50, (f32[1,4,256]{2,1,0:T(4,128)S(1)}, f32[1,4,256]{2,1,0:T(4,128)S(1)}, f32[1,4,256,128]{3,2,1,0:T(8,128)S(1)}) %tuple.106, (s32[]{:T(128)}, s32[1024]{0:T(1024)S(1)}, ...), branch_computations={%region_3.4_spmd, %region_4.7_spmd.clone} | conditional | flops 552881664 | bytes 15572565 | solution.py:110
  380.3 1.8 fusion.2
  382.1 2.4 fusion.12
  386.9 6.2 %conditional.3 = ((f32[1,4,256]{2,1,0:T(4,128)S(1)}, f32[1,4,256]{2,1,0:T(4,128)S(1)}, f32[1,4,256,128]{3,2,1,0:T(8,128)S(1)})) conditional(s32[]{:T(128)} %convert_element_type.50, (f32[1,4,256]{2,1,0:T(4,128)S(1)}, f32[1,4,256]{2,1,0:T(4,128)S(1)}, f32[1,4,256,128]{3,2,1,0:T(8,128)S(1)}) %tuple.106, (s32[]{:T(128)}, s32[1024]{0:T(1024)S(1)}, ...), branch_computations={%region_3.4_spmd, %region_4.7_spmd.clone} | conditional | flops 552881664 | bytes 15572565 | solution.py:110
  387.9 1.8 fusion.2
  389.6 2.4 fusion.12
  393.4 4.8 %convolution_convert_fusion = bf16[256,4096]{1,0:T(8,128)(2,1)} fusion(bf16[256,512]{0,1:T(8,128)(2,1)S(1)} %bitcast.104, bf16[512,4096]{1,0:T(8,128)(2,1)} %param.25), kind=kOutput, calls=%fused_computation.41 | convolution fusion | flops 1074790400 | bytes 6553600 | tf_op jit(solution)/shard_map/dot_general | solution.py:120
  398.2 29.3 %reduce-scatter.2.cloned.1.call-done = bf16[64,4096]{1,0:T(8,128)(2,1)} async-done(((bf16[256,4096]{1,0:T(8,128)(2,1)}), bf16[64,4096]{1,0:T(8,128)(2,1)}) %reduce-scatter.2.cloned.1.call-update) | async-done | bytes 524304 | tf_op jit(solution)/shard_map/reduce_scatter | solution.py:119
  (221 shorter events, 45.1 us)
Async XLA Ops:
  6.5 107.8 %all-gather.8.cloned.1.call-start = ((), (), s32[]{:S(2)}) async-start(), calls=%async_computation.2 | async-start | bytes 17039360 | tf_op jit(solution)/shard_map/all_gather | solution.py:34
  7.3 185.9 %all-gather.10.cloned.1.call-start = ((), (), s32[]{:S(2)}) async-start(), calls=%async_computation.3 | async-start | bytes 4259840 | tf_op jit(solution)/shard_map/all_gather | solution.py:62
  8.0 264.2 %all-gather.6.cloned.1.call-start = ((), (), s32[]{:S(2)}) async-start(), calls=%async_computation.1 | async-start | bytes 4259840 | tf_op jit(solution)/shard_map/all_gather | solution.py:61
  8.7 418.8 %reduce-scatter.2.cloned.1.call-start = ((), (), s32[]{:S(2)}) async-start(), calls=%async_computation.4 | async-start | bytes 2621440 | tf_op jit(solution)/shard_map/reduce_scatter | solution.py:119
Sparse Core Ops, SparseCore 0:
  10.1 104.1 all-gather.7
  117.1 75.9 all-gather.9
  195.9 76.2 all-gather.5
  398.4 29.1 reduce-scatter.1
where the time goes:
time: 436 us; the launch traced here: 434 us
  waiting for transfers between devices  188 us (43%)
  blocking collectives  90.9 us (21%)
  matrix products  71.8 us (16%)
  other arithmetic  46.9 us (11%)
  between operations  13.2 us (3%)
  loops' own time  12.6 us (3%)
  local copies, waits for them, and re-layouts  10.4 us (2%)
    all_gather x1, waiting for transfers between devices, local(): key_piece = lax.all_gather(keys, 'ctx', axis=0, tiled=True)  79.1 us
    all_gather x1, waiting for transfers between devices, local(): value_piece = lax.all_gather(values, 'ctx', axis=0, tiled=True)  71.1 us
    all_gather x1, blocking collectives, local(): lax.all_gather(seg_blocks, 'ctx', axis=0, tiled=True)  48.2 us
    all_gather x1, blocking collectives, local(): seg_piece = lax.all_gather(segments, 'ctx', axis=0, tiled=True)  42.7 us
    dot_general x16, matrix products, update(): jnp.einsum('gcrk,kgd->gcrd', expo.astype(jnp.bfloat16), value_step, prefe...  38.8 us
    reduce_scatter x1, waiting for transfers between devices, local(): lax.psum_scatter(jnp.dot(attn, out_proj, preferred_element_type=jnp.float...  29.3 us
    dot_general x16, matrix products, update(): jnp.einsum('rgcd,kgd->gcrk', query_heads, key_step, preferred_element_typ...  28.2 us
    reduce_sum x16, other arithmetic, update(): new_denom = denom * factor + jnp.sum(expo, axis=-1)  16.6 us
  transfers between devices with their start and end apart: 4, of which 4 were waited for; matrix products, arithmetic and copies ran while one was open for 4% of the time, Pallas kernels for 0%

commit v1 on v0

v1 whole, which is shorter than its diff:
```python
import functools
import math

import jax
import jax.numpy as jnp
from jax import lax
from jax.experimental import pallas as pl
from jax.experimental.pallas import tpu as pltpu
from jax.sharding import PartitionSpec as P

MESH = pl.DeviceIdType.MESH
HD = 128
BLK = 128
GROUP = 4
NX, NZ, CORES = 4, 8, 2
CTX = NX * NZ * CORES
HEADS = 4
ROWS = 256
KSEG = ROWS + 16
PIECE = KSEG + ROWS
DOC_STEP = 32768
MASKED = -1e30
BIAS = -(2**31)
SCALE = math.log2(math.e) / math.sqrt(HD)


def ctx_of(x, z, core):
    return (x * NZ + z) * CORES + core


def ring_offsets(size):
    half = size // 2
    found = [0]
    for step in range(1, half):
        found += [step, -step]
    return found + [half]


def piece_order(size_a, size_b):
    pieces = [(da, db) for da in ring_offsets(size_a) for db in ring_offsets(size_b)]
    return sorted(pieces, key=lambda piece: abs(piece[0]) + abs(piece[1]))


ORDERS = (piece_order(NX, NZ), piece_order(NZ, NX))


class Place:
    def __init__(self):
        ctx = lax.axis_index("ctx")
        self.ctx = ctx
        self.head = lax.axis_index("head")
        self.core = ctx % CORES
        self.z = (ctx // CORES) % NZ
        self.x = ctx // (CORES * NZ)

    def chip(self, dx, dz, core):
        return ctx_of((self.x + dx + NX) % NX, (self.z + dz + NZ) % NZ, core)

    def piece(self, role, da, db):
        dx, dz = (da, db) if role == 0 else (db, da)
        return self.chip(dx, dz, role)

    def device(self, ctx):
        return {"ctx": ctx, "head": self.head}


def gather_attend(
    queries, keys, values, segs, ranges, out,
    held, scaled, total, top, first, width, recv_sem, send_sem,
):
    place = Place()
    me = place.ctx

    barrier = pltpu.get_barrier_semaphore()
    around = [place.device(place.chip(dx, dz, place.core)) for dx, dz in ((1, 0), (-1, 0), (0, 1), (0, -1))]
    around.append(place.device(place.chip(0, 0, 1 - place.core)))
    for device in around:
        pl.semaphore_signal(barrier, inc=1, device_id=device, device_id_type=MESH)

    held[me, 0:ROWS, :] = keys[...]
    seg_rows = segs[...]
    held[me, ROWS:KSEG, :] = jnp.concatenate(
        [seg_rows.astype(jnp.float32), jnp.zeros((14, BLK), jnp.float32)], axis=0
    ).astype(jnp.bfloat16)
    held[me, KSEG:PIECE, :] = values[...]
    pl.semaphore_wait(barrier, len(around))

    parts = {"all": (0, PIECE, 0), "keys": (0, KSEG, 0), "values": (KSEG, ROWS, 1)}

    def copy(part, slot, kind, index, device):
        start, size, which = parts[part]
        rows = held.at[slot, pl.ds(start, size), :]
        return pltpu.make_async_remote_copy(
            src_ref=rows, dst_ref=rows,
            send_sem=send_sem.at[index, kind], recv_sem=recv_sem.at[slot, which],
            device_id=place.device(device), device_id_type=MESH,
        )

    def sends(role, index):
        da, db = ORDERS[role][index]
        size_a, size_b = (NX, NZ) if role == 0 else (NZ, NX)
        slot = place.piece(role, da, db)

        def along(axis, way):
            step = way if axis == 0 else 0, way if axis == 1 else 0
            dx, dz = step if role == 0 else (step[1], step[0])
            return place.chip(dx, dz, role)

        found = []

        def carry(axis, offset, size):
            if offset == 0:
                found.append(("all", slot, 2 * axis, index, along(axis, 1)))
                found.append(("all", slot, 2 * axis + 1, index, along(axis, -1)))
            elif abs(offset) < size // 2:
                way = -1 if offset > 0 else 1
                part = "all" if abs(offset) < size // 2 - 1 else ("keys" if offset > 0 else "values")
                found.append((part, slot, 2 * axis + (0 if way > 0 else 1), index, along(axis, way)))

        if db == 0:
            carry(0, da, size_a)
        carry(1, db, size_b)
        found.append(("all", slot, 4, index, place.chip(0, 0, 1 - role)))
        return found

    def arrive(role, index):
        da, db = ORDERS[role][index]
        size_a, size_b = (NX, NZ) if role == 0 else (NZ, NX)
        slot = place.piece(role, da, db)
        if da == 0 and db == 0:
            return
        halves = db == size_b // 2 or (db == 0 and da == size_a // 2)
        for part in ("keys", "values") if halves else ("all",):
            copy(part, slot, 0, index, me).wait_recv()

    def events(step):
        for role in range(2):
            for count in range(len(ORDERS[role]) // 2):

                @pl.when((place.core == role) & (step == count))
                def _(role=role, count=count):
                    for index in (2 * count, 2 * count + 1):
                        arrive(role, index)
                        for each in sends(role, index):
                            copy(*each).start()

    def slot_of(role_is, index):
        offsets = []
        for axis in range(2):
            value = jnp.int32(0)
            for role in range(2):
                for place_in in range(len(ORDERS[role])):
                    amount = ORDERS[role][place_in]
                    dx, dz = amount if role == 0 else (amount[1], amount[0])
                    value = jnp.where(
                        (role_is == role) & (index == place_in), (dx, dz)[axis], value
                    )
            offsets.append(value)
        return place.chip(offsets[0], offsets[1], role_is)

    events(jnp.int32(0))

    bounds = ranges[pl.ds(2 * me, 2), :]
    for block in range(2):
        low, high, causal = (bounds[block : block + 1, i : i + 1] for i in range(3))
        seg = jnp.transpose(
            jnp.broadcast_to(seg_rows[block : block + 1, :].astype(jnp.float32), (BLK, BLK))
        ).astype(jnp.int32)
        pos = me * ROWS + block * BLK + lax.broadcasted_iota(jnp.int32, (BLK, BLK), 0)
        start = jnp.broadcast_to(low * BLK, (BLK, BLK))
        end = jnp.broadcast_to(high * BLK + (BLK - 1), (BLK, BLK))
        end = jnp.where(jnp.broadcast_to(causal, (BLK, BLK)) == 0, end, jnp.minimum(end, pos))
        first[block * BLK : (block + 1) * BLK, :] = jnp.int32(BIAS) - (start + seg * DOC_STEP)
        width[block * BLK : (block + 1) * BLK, :] = (end - start + 1) + jnp.int32(BIAS)

    for head in range(GROUP):
        query = queries[:, head * HD : (head + 1) * HD].astype(jnp.float32) * SCALE
        large = query.astype(jnp.bfloat16)
        scaled[head, :, 0:HD] = large
        scaled[head, :, HD : 2 * HD] = (query - large.astype(jnp.float32)).astype(jnp.bfloat16)
    top[...] = jnp.full(top.shape, MASKED, jnp.float32)
    total[...] = jnp.zeros(total.shape, jnp.float32)

    def attend(slots):
        lines, key_parts, value_parts = [], [], []
        lane = lax.broadcasted_iota(jnp.int32, (1, BLK), 1)
        for slot in slots:
            key = held[slot, 0:ROWS, :]
            key_parts.append(jnp.concatenate([key, key], axis=1))
            value = held[slot, KSEG:PIECE, :]
            value_parts.append(jnp.concatenate([value, jnp.ones_like(value)], axis=1))
            docs = held[slot, ROWS:KSEG, :].astype(jnp.float32).astype(jnp.int32)
            for block in range(2):
                lines.append(docs[block : block + 1, :] * DOC_STEP + lane + (slot * ROWS + block * BLK))
        value_all = jnp.concatenate(value_parts, axis=0)
        for head in range(GROUP):
            scores = []
            for at, key in enumerate(key_parts):
                score = lax.dot_general(
                    scaled[head], key, (((1,), (1,)), ((), ())), preferred_element_type=jnp.float32
                )
                for block in range(2):
                    inside = lines[2 * at + block] + first[...] < width[...]
                    scores.append(jnp.where(inside, score[:, block * BLK : (block + 1) * BLK], MASKED))
            largest = functools.reduce(jnp.maximum, scores)
            old = top[head]
            new = jnp.maximum(old, jnp.max(largest, axis=1, keepdims=True))
            top[head] = new
            factor = jnp.exp2(old - new)
            expo = jnp.concatenate([jnp.exp2(score - new).astype(jnp.bfloat16) for score in scores], axis=1)
            added = jnp.dot(expo, value_all, preferred_element_type=jnp.float32)
            total[head, :, 0:HD] = total[head, :, 0:HD] * factor + added[:, 0:HD]
            total[head, :, HD : 2 * HD] = total[head, :, HD : 2 * HD] * factor + added[:, HD : 2 * HD]

    steps = len(ORDERS[0]) // 2

    def one_step(step, carry):
        events(step + 1)
        slots = []
        for index in range(2):
            slots.append(slot_of(place.core, 2 * step + index))
            other = slot_of(1 - place.core, 2 * step + index)
            copy("all", other, 0, 0, me).wait_recv()
            slots.append(other)
        attend(slots)
        return carry

    lax.fori_loop(0, steps, one_step, 0)

    for head in range(GROUP):
        out[:, head * HD : (head + 1) * HD] = (
            total[head, :, 0:HD] / total[head, :, HD : 2 * HD]
        ).astype(jnp.bfloat16)

    for role in range(2):

        @pl.when(place.core == role)
        def _(role=role):
            for index in range(len(ORDERS[role])):
                for each in sends(role, index):
                    copy(*each).wait_send()


def call_gather_attend(queries, keys, values, segs, ranges):
    vmem = pl.BlockSpec(memory_space=pltpu.VMEM)
    flops = 4 * GROUP * ROWS * ROWS * CTX * HD
    return pl.pallas_call(
        gather_attend,
        out_shape=jax.ShapeDtypeStruct((ROWS, GROUP * HD), jnp.bfloat16),
        in_specs=[vmem] * 5,
        out_specs=vmem,
        scratch_shapes=[
            pltpu.VMEM((CTX, PIECE, HD), jnp.bfloat16),
            pltpu.VMEM((GROUP, ROWS, 2 * HD), jnp.bfloat16),
            pltpu.VMEM((GROUP, ROWS, 2 * HD), jnp.float32),
            pltpu.VMEM((GROUP, ROWS, HD), jnp.float32),
            pltpu.VMEM((ROWS, BLK), jnp.int32),
            pltpu.VMEM((ROWS, BLK), jnp.int32),
            pltpu.SemaphoreType.DMA((CTX, 2)),
            pltpu.SemaphoreType.DMA((NX * NZ, 5)),
        ],
        compiler_params=pltpu.CompilerParams(
            collective_id=0, has_side_effects=True, vmem_limit_bytes=48 << 20
        ),
        cost_estimate=pl.CostEstimate(
            flops=flops, bytes_accessed=CTX * PIECE * HD * 2, transcendentals=GROUP * ROWS * ROWS * CTX
        ),
        name="gather_attend",
    )(queries, keys, values, segs, ranges)


def local(queries, keys, values, segments, block_ranges, owner, out_proj):
    attn = call_gather_attend(queries, keys, values, segments.reshape(2, BLK), block_ranges)
    lead = attn.reshape(2, CTX, 2, GROUP * HD).transpose(1, 0, 2, 3).reshape(CTX, 4, GROUP * HD)
    spread = lax.all_to_all(lead, "ctx", 0, 0, tiled=True).reshape(CTX, 2, 2, GROUP * HD)
    owners = owner.reshape(CTX, 2)
    home = jnp.argmax(owners[None, :, :] == jnp.arange(CTX, dtype=jnp.int32)[:, None, None], axis=1)
    moved = jnp.stack([jnp.take(spread[:, j], home[:, j], axis=0) for j in range(2)], axis=1)
    owned = lax.all_to_all(moved.reshape(CTX, 4, GROUP * HD), "ctx", 0, 0, tiled=True)
    owned = owned.reshape(CTX, 2, 2, GROUP * HD).transpose(1, 0, 2, 3).reshape(ROWS, GROUP * HD)
    product = jnp.dot(owned, out_proj, preferred_element_type=jnp.float32).astype(jnp.bfloat16)
    return lax.psum_scatter(product, "head", scatter_dimension=0, tiled=True)


def solution(mesh):
    return jax.shard_map(
        local,
        mesh=mesh,
        in_specs=(
            P("ctx", "head"),
            P("ctx", "head"),
            P("ctx", "head"),
            P("ctx"),
            P(),
            P(),
            P("head", None),
        ),
        out_specs=P(("ctx", "head"), None),
        check_vma=False,
    )
```

time: 436 us -> 172 us (0.39)
  waiting for transfers between devices: 188 us -> 40.4 us
  Pallas kernels: 0 us -> 76.6 us
  blocking collectives: 90.9 us -> 17.8 us
  matrix products: 71.8 us -> 4.8 us
  other arithmetic: 46.9 us -> 1.46 us
  loops' own time: 12.6 us -> 0 us
  starting transfers between devices: 0.12 us -> 8.62 us
    all_gather x3 -> x0, waiting for transfers between devices: 157 us -> none  [the longest x1 79.1 us: local(): key_piece = lax.all_gather(keys, 'ctx', axis=0, tiled=True)]
    all_gather x2 -> x0, blocking collectives: 90.9 us -> none  [the longest x1 48.2 us: local(): lax.all_gather(seg_blocks, 'ctx', axis=0, tiled=True)]
    pallas_call x0 -> x1, Pallas kernels: none -> 76.6 us  [call_gather_attend(): pl.pallas_call(gather_attend, out_shape=jax.ShapeDtypeStruct((ROWS, GROUP...]
    dot_general x33 -> x1, matrix products: 71.8 us -> 4.8 us  [local(): jnp.dot(owned, out_proj, preferred_element_type=jnp.float32)]
    all_to_all x0 -> x1, blocking collectives: none -> 17.8 us  [local(): lax.all_to_all(moved.reshape(CTX, 4, GROUP * HD), 'ctx', 0, 0, tiled=True)]
    reduce_sum x17 -> x0, other arithmetic: 16.7 us -> none  [the longest x16 16.6 us: update(): new_denom = denom * factor + jnp.sum(expo, axis=-1)]
    another operation x17 -> x0, loops' own time: 12.6 us -> none  [the longest x1 11.3 us: local(): lax.fori_loop(0, piece_len // width, one_step, start_state)]
    and x17 -> x1, other arithmetic: 12.3 us -> 0.01 us  [local(): jnp.take(spread[:, j], home[:, j], axis=0)]
  transfers between devices with their start and end apart: 4 -> 2, of which waited for: 4 -> 2; matrix products, arithmetic and copies ran while one was open for 4% -> 1% of each run, Pallas kernels for 0% -> 0%
where the time goes in v1:
time: 172 us; the launch traced here: 171 us
  Pallas kernels  76.6 us (45%)
  waiting for transfers between devices  40.4 us (23%)
  blocking collectives  17.8 us (10%)
  between operations  13.5 us (8%)
  starting transfers between devices  8.62 us (5%)
  local copies, waits for them, and re-layouts  7.97 us (5%)
  matrix products  4.8 us (3%)
    pallas_call x1, Pallas kernels, call_gather_attend(): pl.pallas_call(gather_attend, out_shape=jax.ShapeDtypeStruct((ROWS, GROUP...  76.6 us
    reduce_scatter x1, waiting for transfers between devices, local(): return lax.psum_scatter(product, 'head', scatter_dimension=0, tiled=True)  29.3 us
    all_to_all x1, blocking collectives, local(): lax.all_to_all(moved.reshape(CTX, 4, GROUP * HD), 'ctx', 0, 0, tiled=True)  17.8 us
    all_to_all x1, waiting for transfers between devices, local(): lax.all_to_all(lead, 'ctx', 0, 0, tiled=True).reshape(CTX, 2, 2, GROUP * HD)  11 us
    all_to_all x1, starting transfers between devices, local(): lax.all_to_all(lead, 'ctx', 0, 0, tiled=True).reshape(CTX, 2, 2, GROUP * HD)  8.58 us
    dot_general x1, matrix products, local(): jnp.dot(owned, out_proj, preferred_element_type=jnp.float32)  4.8 us
    unnamed x11, local copies, waits for them, and re-layouts  4.09 us
  transfers between devices with their start and end apart: 2, of which 2 were waited for; matrix products, arithmetic and copies ran while one was open for 1% of the time, Pallas kernels for 0%

profile of v1, /device:TPU:1, one launch (start us, length us, event | category | flops | bytes accessed | tf_op | source)
XLA Modules:
  0.0 171.2 jit_solution(11844119239059172101)
XLA Ops:
  6.5 0.8 copy.42.ranges
  7.3 0.0 copy-start
  7.3 0.9 copy-done
  8.3 0.0 copy-start.1
  8.3 0.8 copy-done.1
  9.1 0.0 copy-start.2
  9.1 0.8 copy-done.2
  10.0 0.0 copy-start.3
  10.0 0.7 copy-done.3
  10.6 0.0 copy-start.4
  10.6 76.6 %gather_attend.1 = bf16[256,512]{1,0:T(8,128)(2,1)S(1)} custom-call(bf16[256,512]{1,0:T(8,128)(2,1)S(1)} %copy-done, bf16[256,128]{1,0:T(8,128)(2,1)S(1)} %copy-done.1, bf16[256,128]{1,0:T(8,128)(2,1)S(1)} %copy-done.2, s32[2,128]{1,0:T(2,128)S(1)} %bitcast.25, s32[128,3]{1,0:T(8,128)S(1)} %copy.42.ranges), custom_call_target="tpu_custom_call" | custom-call | flops 8589934592 | bytes 8650752 | tf_op jit(solution)/shard_map/gather_attend/pallas_call | solution.py:247
  87.3 0.1 reshape.28
  87.4 0.9 copy.44
  88.3 8.6 %all-to-all-start = ((bf16[64,4,512]{2,1,0:T(4,128)(2,1)}), bf16[64,4,512]{2,1,0:T(4,128)(2,1)S(1)}, u32[]{:S(2)}, u32[]{:S(2)}) async-start(bf16[64,4,512]{2,1,0:T(4,128)(2,1)} %copy.44), calls=%async_computation | async-start | bytes 524288 | tf_op jit(solution)/shard_map/all_to_all | solution.py:275
  96.9 0.0 reduce-scatter.2.cloned.1.call-start
  97.0 0.0 copy-done.4
  97.0 0.1 eq.17
  97.1 0.1 copy.41
  97.2 0.7 iota_reduce_fusion
  97.9 11.0 %all-to-all-done = bf16[64,4,512]{2,1,0:T(4,128)(2,1)S(1)} async-done(((bf16[64,4,512]{2,1,0:T(4,128)(2,1)}), bf16[64,4,512]{2,1,0:T(4,128)(2,1)S(1)}, u32[]{:S(2)}, u32[]{:S(2)}) %all-to-all-start) | async-done | bytes 262176 | tf_op jit(solution)/shard_map/all_to_all | solution.py:275
  109.0 0.3 copy_bitcast_fusion.1
  109.3 0.8 gather_fusion.1
  110.1 0.2 fusion.1
  110.3 0.8 gather_fusion
  111.2 0.2 fusion
  111.4 0.4 pad_maximum_fusion
  111.8 0.2 copy.49
  112.0 17.8 %all_to_all.10 = bf16[64,4,512]{2,1,0:T(4,128)(2,1)S(1)} all-to-all(bf16[64,4,512]{2,1,0:T(4,128)(2,1)S(1)} %copy.49), channel_id=1, replica_groups=mesh['ctx'=64,'head'=4] {'ctx'}, dimensions={0} | all-to-all | bytes 524288 | tf_op jit(solution)/shard_map/all_to_all | solution.py:279
  129.8 0.1 reshape.32
  129.9 0.2 copy.56
  130.1 0.1 reshape.33
  130.2 4.8 %convolution_convert_fusion = bf16[256,4096]{1,0:T(8,128)(2,1)} fusion(bf16[256,512]{1,0:T(8,128)(2,1)S(1)} %reshape.33, bf16[512,4096]{1,0:T(8,128)(2,1)} %param.15), kind=kOutput, calls=%fused_computation.2 | convolution fusion | flops 1074790400 | bytes 6553600 | tf_op jit(solution)/shard_map/dot_general | solution.py:281
  135.0 0.0 reduce-scatter.2.cloned.1.call-update
  135.1 29.3 %reduce-scatter.2.cloned.1.call-done = bf16[64,4096]{1,0:T(8,128)(2,1)} async-done(((bf16[256,4096]{1,0:T(8,128)(2,1)}), bf16[64,4096]{1,0:T(8,128)(2,1)}) %reduce-scatter.2.cloned.1.call-update) | async-done | bytes 524304 | tf_op jit(solution)/shard_map/reduce_scatter | solution.py:282
  (6 shorter events, 0.1 us)
Async XLA Ops:
  7.3 0.9 copy-start
  8.3 0.8 copy-start.1
  9.1 0.8 copy-start.2
  10.0 0.7 copy-start.3
  10.6 86.3 %copy-start.4 = (s32[128]{0:T(128)S(1)}, s32[128]{0:T(128)}, u32[]{:S(2)}) copy-start(s32[128]{0:T(128)} %param.14) | copy-start | bytes 1540
  88.3 20.6 %all-to-all-start = ((bf16[64,4,512]{2,1,0:T(4,128)(2,1)}), bf16[64,4,512]{2,1,0:T(4,128)(2,1)S(1)}, u32[]{:S(2)}, u32[]{:S(2)}) async-start(bf16[64,4,512]{2,1,0:T(4,128)(2,1)} %copy.44), calls=%async_computation | async-start | bytes 524288 | tf_op jit(solution)/shard_map/all_to_all | solution.py:275
  96.9 67.4 %reduce-scatter.2.cloned.1.call-start = ((), (), s32[]{:S(2)}) async-start(), calls=%async_computation.3 | async-start | bytes 2621440 | tf_op jit(solution)/shard_map/reduce_scatter | solution.py:282
Sparse Core Ops, SparseCore 0:
  135.2 29.1 reduce-scatter.1

commit v2 on v1

v2 whole, which is shorter than its diff:
```python
import functools
import math

import jax
import jax.numpy as jnp
from jax import lax
from jax.experimental import pallas as pl
from jax.experimental.pallas import tpu as pltpu
from jax.sharding import PartitionSpec as P

MESH = pl.DeviceIdType.MESH
HD = 128
BLK = 128
GROUP = 4
NX, NZ, CORES = 4, 8, 2
CTX = NX * NZ * CORES
HEADS = 4
ROWS = 256
KSEG = ROWS + 16
PIECE = KSEG + ROWS
CHIPS = NX * NZ
WIDE = 4096
HALF = WIDE // 2
TURN = 32
MIXED = CHIPS * 16
CLASSES = 16
TRIPLE = 3
LOOKAHEAD = 1
DOC_STEP = 32768
MASKED = -1e30
SCALE = math.log2(math.e) / math.sqrt(HD)


def ctx_of(x, z, core):
    return (x * NZ + z) * CORES + core


def ring_offsets(size):
    half = size // 2
    found = [0]
    for step in range(1, half):
        found += [step, -step]
    return found + [half]


def piece_order(size_a, size_b):
    pieces = [(da, db) for da in ring_offsets(size_a) for db in ring_offsets(size_b)]
    return sorted(pieces, key=lambda piece: abs(piece[0]) + abs(piece[1]))


ORDERS = (piece_order(NX, NZ), piece_order(NZ, NX))


class Place:
    def __init__(self):
        ctx = lax.axis_index("ctx")
        self.ctx = ctx
        self.head = lax.axis_index("head")
        self.core = ctx % CORES
        self.z = (ctx // CORES) % NZ
        self.x = ctx // (CORES * NZ)
        self.chip_here = ctx // CORES

    def chip(self, dx, dz, core):
        return ctx_of((self.x + dx + NX) % NX, (self.z + dz + NZ) % NZ, core)

    def device(self, ctx):
        return {"ctx": ctx, "head": self.head}

    def plane(self, step):
        return (self.head + step) % HEADS


def iota(shape, dim):
    return lax.broadcasted_iota(jnp.int32, shape, dim)


def one_hot(mask):
    return jnp.where(mask, 1.0, 0.0).astype(jnp.bfloat16)


def exact(left, right):
    return jnp.dot(left, right, preferred_element_type=jnp.float32)


def kernel(
    queries_hbm, keys_hbm, values_hbm, segs_hbm, ranges_hbm, owner_hbm, proj_hbm, out,
    queries, keys, segs, ranges, owner, proj, load_sem,
    held, scaled, total, top, recv_sem, send_sem,
    attn, swap_out, swap_in, spread_out, spread_in, back_in, mix, owned, swap_send, swap_recv, spread_send, spread_recv,
    part, first_in, last_in, sum_send, sum_recv,
):
    place = Place()
    me, core, other = place.ctx, place.core, 1 - place.core

    loads = [
        pltpu.make_async_copy(source, target, load_sem.at[at])
        for at, (source, target) in enumerate(
            (
                (keys_hbm, keys),
                (segs_hbm, segs),
                (values_hbm, held.at[core, 0, pl.ds(KSEG, ROWS), :]),
                (queries_hbm, queries),
                (ranges_hbm, ranges),
                (owner_hbm, owner),
                (proj_hbm, proj),
            )
        )
    ]
    for load in loads:
        load.start()

    barrier = pltpu.get_barrier_semaphore()
    sibling = place.device(place.chip(0, 0, other))

    def greet(step, carry):
        target = place.device(place.chip(step // NZ, step % NZ, core))
        pl.semaphore_signal(barrier, inc=1, device_id=target, device_id_type=MESH)
        return carry

    lax.fori_loop(1, CHIPS, greet, 0)
    pl.semaphore_signal(barrier, inc=1, device_id=sibling, device_id_type=MESH)
    for step in (1, -1):
        pl.semaphore_signal(
            barrier, inc=1, device_id={"ctx": me, "head": place.plane(step)}, device_id_type=MESH
        )

    for load in loads[:3]:
        load.wait()
    for block in range(2):
        turned = jnp.transpose(keys[block * BLK : (block + 1) * BLK, :].astype(jnp.float32))
        held[core, 0, block * BLK : (block + 1) * BLK, :] = turned.astype(jnp.bfloat16)
    seg_rows = segs[...].astype(jnp.float32)
    held[core, 0, ROWS:KSEG, :] = jnp.concatenate(
        [seg_rows, jnp.full((1, BLK), me, jnp.int32).astype(jnp.float32), jnp.zeros((13, BLK), jnp.float32)], axis=0
    ).astype(jnp.bfloat16)
    pl.semaphore_wait(barrier, CHIPS - 1 + 1 + 2)

    parts = {"all": (0, PIECE, 0), "keys": (0, KSEG, 0), "values": (KSEG, ROWS, 1)}

    def copy(piece, name, kind, at, device):
        role, index = piece
        start, size, which = parts[name]
        return pltpu.make_async_remote_copy(
            src_ref=held.at[role, index, pl.ds(start, size), :],
            dst_ref=held.at[role, at, pl.ds(start, size), :],
            send_sem=send_sem.at[index, kind], recv_sem=recv_sem.at[role, at, which],
            device_id=place.device(device), device_id_type=MESH,
        )

    def sends(role, index):
        order = ORDERS[role]
        sizes = (NX, NZ) if role == 0 else (NZ, NX)
        offsets = order[index]
        found = []

        def go(name, axis, way):
            moved = list(offsets)
            moved[axis] -= way
            for each in range(2):
                if moved[each] <= -sizes[each] // 2:
                    moved[each] += sizes[each]
            step = [0, 0]
            step[axis] = way
            dx, dz = step if role == 0 else step[::-1]
            kind = 2 * axis + (0 if way > 0 else 1)
            found.append(copy((role, index), name, kind, order.index(tuple(moved)), place.chip(dx, dz, role)))

        for axis in range(2):
            if axis == 0 and offsets[1] != 0:
                continue
            offset, half = offsets[axis], sizes[axis] // 2
            if offset == 0:
                go("all", axis, 1)
                go("all", axis, -1)
            elif abs(offset) < half:
                name = "all" if abs(offset) < half - 1 else ("keys" if offset > 0 else "values")
                go(name, axis, -1 if offset > 0 else 1)
        found.append(copy((role, index), "all", 4, index, place.chip(0, 0, 1 - role)))
        return found

    def arrive(role, index):
        da, db = ORDERS[role][index]
        sizes = (NX, NZ) if role == 0 else (NZ, NX)
        if index == 0:
            return
        halves = db == sizes[1] // 2 or (db == 0 and da == sizes[0] // 2)
        for name in ("keys", "values") if halves else ("all",):
            copy((role, index), name, 0, index, me).wait_recv()

    def forward(indices):
        for role in range(2):

            @pl.when(core == role)
            def _(role=role):
                for index in indices:
                    arrive(role, index)
                    for each in sends(role, index):
                        each.start()

    forward((0,))

    for load in loads[3:6]:
        load.wait()
    lane = iota((1, BLK), 1)
    bounds = []
    for block in range(2):
        picked = jnp.where(lane == 2 * me + block, ranges[...], 0).astype(jnp.float32)
        bounds.append(jnp.sum(picked, axis=1, keepdims=True).astype(jnp.int32))
    row = iota((CLASSES, BLK), 0)
    low, high = (
        jnp.where(
            row < 3,
            jnp.broadcast_to(bounds[0][at : at + 1, :], (CLASSES, BLK)),
            jnp.broadcast_to(bounds[1][at : at + 1, :], (CLASSES, BLK)),
        )
        for at in range(2)
    )
    class_seg = jnp.where(row < 3, row, row - 3) * DOC_STEP
    class_from = low * BLK + class_seg
    class_to = high * BLK + (BLK - 1) + class_seg

    row_seg = [
        jnp.transpose(jnp.broadcast_to(seg_rows[block : block + 1, :], (BLK, BLK))).astype(jnp.int32)
        for block in range(2)
    ]
    row_class = jnp.concatenate([row_seg[0], row_seg[1] + 3], axis=0)
    chosen = one_hot(row_class[:, 0:CLASSES] == iota((ROWS, CLASSES), 1))
    for head in range(GROUP):
        rows = slice(head * ROWS, (head + 1) * ROWS)
        scaled[rows, 0:HD] = queries[:, head * HD : (head + 1) * HD]
        scaled[rows, HD : HD + CLASSES] = chosen

    def with_ones(value):
        return jnp.concatenate([value, jnp.ones_like(value)], axis=1)

    def line_of(role, index):
        info = held[role, index, ROWS:KSEG, :].astype(jnp.float32).astype(jnp.int32)
        base = info[2:3, :] * ROWS + lane
        return [info[block : block + 1, :] * DOC_STEP + base + block * BLK for block in range(2)]

    own_key = jnp.concatenate([held[core, 0, 0:BLK, :], held[core, 0, BLK : 2 * BLK, :]], axis=1)
    own_value = with_ones(held[core, 0, KSEG:PIECE, :])
    own_line = jnp.concatenate(line_of(core, 0), axis=1)
    inside = []
    for block in range(2):
        low, high, causal = (jnp.broadcast_to(bounds[block][i : i + 1, :], (BLK, BLK)) for i in range(3))
        pos = me * ROWS + block * BLK + iota((BLK, BLK), 0)
        end = high * BLK + (BLK - 1)
        end = jnp.where(causal == 0, end, jnp.minimum(end, pos)) + row_seg[block] * DOC_STEP
        start = low * BLK + row_seg[block] * DOC_STEP
        wide = jnp.broadcast_to(own_line, (BLK, ROWS))
        inside.append(
            (wide >= jnp.concatenate([start, start], axis=1)) & (wide <= jnp.concatenate([end, end], axis=1))
        )
    hidden = jnp.where(jnp.concatenate(inside, axis=0), 0.0, MASKED)
    for head in range(GROUP):
        rows = slice(head * ROWS, (head + 1) * ROWS)
        score = exact(scaled[rows, 0:HD], own_key)
        score = jnp.where(hidden < 0.0, MASKED, score)
        new = jnp.broadcast_to(jnp.max(score, axis=1, keepdims=True), (ROWS, HD))
        top[rows, :] = new
        expo = jnp.concatenate(
            [jnp.exp2((score[:, at * BLK : (at + 1) * BLK] - new) * SCALE).astype(jnp.bfloat16) for at in range(2)],
            axis=1,
        )
        total[rows, :] = exact(expo, own_value)

    def attend(pieces):
        key_parts, value_parts = [], []
        for role, index in pieces:
            blocks = []
            for block, line in enumerate(line_of(role, index)):
                spot = jnp.broadcast_to(line, (CLASSES, BLK))
                seen = (spot >= class_from) & (spot <= class_to)
                extra = jnp.where(seen, 0.0, MASKED).astype(jnp.bfloat16)
                blocks.append(
                    jnp.concatenate([held[role, index, block * BLK : (block + 1) * BLK, :], extra], axis=0)
                )
            key_parts.append(jnp.concatenate(blocks, axis=1))
            value_parts.append(with_ones(held[role, index, KSEG:PIECE, :]))
        value_all = jnp.concatenate(value_parts, axis=0)
        for head in range(GROUP):
            rows = slice(head * ROWS, (head + 1) * ROWS)
            scores = []
            for key in key_parts:
                score = exact(scaled[rows, 0 : HD + CLASSES], key)
                scores += [score[:, 0:BLK], score[:, BLK : 2 * BLK]]
            largest = functools.reduce(jnp.maximum, scores)
            old = top[rows, :]
            new = jnp.maximum(old, jnp.max(largest, axis=1, keepdims=True))
            top[rows, :] = new
            factor = jnp.exp2((old - new) * SCALE)
            expo = jnp.concatenate(
                [jnp.exp2((score - new) * SCALE).astype(jnp.bfloat16) for score in scores], axis=1
            )
            added = exact(expo, value_all)
            total[rows, 0:HD] = total[rows, 0:HD] * factor + added[:, 0:HD]
            total[rows, HD : 2 * HD] = total[rows, HD : 2 * HD] * factor + added[:, HD : 2 * HD]

    steps = (2 * CHIPS - 1) // TRIPLE
    reached = [0]
    for step in range(steps):
        reached.append(min(CHIPS - 1, (TRIPLE * step + 3) // 2 + LOOKAHEAD))
    reached[-1] = CHIPS - 1

    def events(step, low, high):
        if high - low == 1:
            indices = tuple(range(reached[low] + 1, reached[low + 1] + 1))
            if indices:
                forward(indices)
            return
        middle = (low + high) // 2

        @pl.when(step < middle)
        def _():
            events(step, low, middle)

        @pl.when(step >= middle)
        def _():
            events(step, middle, high)

    def one_step(step, carry):
        events(step, 0, steps)
        pieces = []
        for each in range(TRIPLE):
            at = TRIPLE * step + each
            own = at % 2
            role, index = (core + 1 + own) % 2, (at + own) // 2

            @pl.when(own == 0)
            def _(role=role, index=index):
                copy((role, index), "all", 0, index, me).wait_recv()

            pieces.append((role, index))
        attend(pieces)
        return carry

    lax.fori_loop(0, steps, one_step, 0)

    for role in range(2):

        @pl.when(core == role)
        def _(role=role):
            for index in range(CHIPS):
                for each in sends(role, index):
                    each.wait_send()

    for head in range(GROUP):
        rows = slice(head * ROWS, (head + 1) * ROWS)
        attn[head] = (total[rows, 0:HD] / total[rows, HD : 2 * HD]).astype(jnp.bfloat16)

    at_out, at_in = iota((ROWS, ROWS), 0), iota((ROWS, ROWS), 1)
    scatter_rows = one_hot(at_in == (at_out % 8) * TURN + at_out // 8)
    gather_rows = one_hot(at_in == (at_out % TURN) * 8 + ((at_out % 64) // TURN) * GROUP + at_out // 64)

    def swap(turn, way):
        return pltpu.make_async_remote_copy(
            src_ref=swap_out.at[way, turn], dst_ref=swap_in.at[way, turn],
            send_sem=swap_send.at[way, turn], recv_sem=swap_recv.at[way, turn],
            device_id=sibling, device_id_type=MESH,
        )

    def spread(turn, way):
        target = spread_in if way == 0 else back_in

        def one(step, carry):
            there = ctx_of((place.x + step // NZ) % NX, (place.z + step % NZ) % NZ, core)
            pltpu.make_async_remote_copy(
                src_ref=spread_out.at[way, turn, there // CORES], dst_ref=target.at[turn, place.chip_here],
                send_sem=spread_send.at[way, turn], recv_sem=spread_recv.at[way, turn],
                device_id=place.device(there), device_id_type=MESH,
            ).start()
            return carry

        lax.fori_loop(1, CHIPS, one, 0)
        target[turn, place.chip_here] = spread_out[way, turn, place.chip_here]

    def spread_arrived(turn, way):
        target = spread_in if way == 0 else back_in
        many = target.at[turn, pl.ds(0, CHIPS - 1)]
        pltpu.make_async_copy(many, many, spread_recv.at[way, turn]).wait()

    def spread_sent(turn, way):
        many = spread_out.at[way, turn, pl.ds(0, CHIPS - 1)]
        pltpu.make_async_copy(many, many, spread_send.at[way, turn]).wait()

    for turn in range(2):
        for block in range(2):
            planes = [
                attn[head, block * BLK + 64 * side + TURN * turn : block * BLK + 64 * side + TURN * (turn + 1), :]
                for side in range(2)
                for head in range(GROUP)
            ]
            dealt = exact(scatter_rows, jnp.concatenate(planes, axis=0)).astype(jnp.bfloat16)
            owned[turn, block] = dealt
        swap_out[0, turn] = owned[turn, other]
        swap(turn, 0).start()

    def block_core(at):
        return jnp.where((at % 16) // 8 == 0, core, other)

    came = iota((BLK, MIXED), 1)
    expand = one_hot(iota((BLK, MIXED), 0) == 2 * (2 * (came // 16) + block_core(came)) + core)
    owner_rows = jnp.broadcast_to(owner[...].astype(jnp.float32), (8, BLK)).astype(jnp.bfloat16)
    owner_of = exact(owner_rows, expand)[0:1, :].astype(jnp.int32)
    code_in = owner_of * 8 + iota((1, MIXED), 1) % 8
    leaves = iota((MIXED, BLK), 0)
    code_out = (2 * (leaves // 16) + block_core(leaves)) * 8 + leaves % 8
    for at in range(MIXED // BLK):
        columns = slice(at * BLK, (at + 1) * BLK)
        mix[:, columns] = one_hot(code_out == jnp.broadcast_to(code_in[:, columns], (MIXED, BLK)))

    def eights(rows):
        return rows.astype(jnp.float32).reshape(CHIPS, 8, HD)

    for turn in range(2):
        swap(turn, 0).wait_recv()
        both = jnp.concatenate([eights(owned[turn, core]), eights(swap_in[0, turn])], axis=1)
        spread_out[0, turn] = both.astype(jnp.bfloat16)
        spread(turn, 0)
    for turn in range(2):
        spread_arrived(turn, 0)
        came_rows = spread_in[turn].reshape(MIXED, HD)
        spread_out[1, turn] = exact(mix[...], came_rows).astype(jnp.bfloat16).reshape(CHIPS, 16, HD)
        spread(turn, 1)
    for turn in range(2):
        spread_arrived(turn, 1)
        landed = back_in[turn].astype(jnp.float32)
        owned[turn, core] = landed[:, 0:8, :].reshape(ROWS, HD).astype(jnp.bfloat16)
        swap_out[1, turn] = landed[:, 8:16, :].reshape(ROWS, HD).astype(jnp.bfloat16)
        swap(turn, 1).start()

    def give(turn, message):
        way = 1 if message % 2 == 0 else -1
        side = (0, 1, 1, 0, 0, 1)[message]
        dest = place.plane(2 if message < 2 else way)
        if message < 2:
            target = first_in.at[turn, message]
        else:
            target = last_in.at[turn, message % 2, side]
        return pltpu.make_async_remote_copy(
            src_ref=part.at[turn, dest, side], dst_ref=target,
            send_sem=sum_send.at[turn, message], recv_sem=sum_recv.at[turn, message],
            device_id={"ctx": me, "head": place.plane(way)}, device_id_type=MESH,
        )

    loads[6].wait()
    for turn in range(2):
        swap(turn, 1).wait_recv()
        owned[turn, other] = swap_in[1, turn]
        lefts = []
        for block in range(2):
            sorted_rows = exact(gather_rows, owned[turn, block]).astype(jnp.bfloat16)
            lefts.append(jnp.concatenate([sorted_rows[64 * head : 64 * (head + 1), :] for head in range(GROUP)], axis=1))
        left = jnp.concatenate(lefts, axis=0)
        for side in range(2):
            for at in range(2):
                start = side * HALF + at * (HALF // 2)
                product = exact(left, proj[:, start : start + HALF // 2]).astype(jnp.bfloat16)
                for dest in range(HEADS):
                    part[turn, dest, side, :, at * (HALF // 2) : (at + 1) * (HALF // 2)] = product[
                        dest * TURN : (dest + 1) * TURN, :
                    ]
        for message in range(4):
            give(turn, message).start()
    for turn in range(2):
        for message in (4, 5):
            way = 1 if message == 4 else -1
            side = message - 4
            give(turn, message - 4).wait_recv()
            dest = place.plane(way)
            merged = part[turn, dest, side].astype(jnp.float32) + first_in[turn, side].astype(jnp.float32)
            part[turn, dest, side] = merged.astype(jnp.bfloat16)
            give(turn, message).start()
    for turn in range(2):
        for message in range(2, 6):
            give(turn, message).wait_recv()
        for side in range(2):
            summed = part[turn, place.head, side].astype(jnp.float32)
            for way in range(2):
                summed = summed + last_in[turn, way, side].astype(jnp.float32)
            out[turn * TURN : (turn + 1) * TURN, side * HALF : (side + 1) * HALF] = summed.astype(jnp.bfloat16)

    for turn in range(2):
        for way in range(2):
            swap(turn, way).wait_send()
            spread_sent(turn, way)
        for message in range(6):
            give(turn, message).wait_send()


def local(queries, keys, values, segments, block_ranges, owner, out_proj):
    anywhere = pl.BlockSpec(memory_space=pl.ANY)
    bf16, i32, f32 = jnp.bfloat16, jnp.int32, jnp.float32
    dma = pltpu.SemaphoreType.DMA
    return pl.pallas_call(
        kernel,
        out_shape=jax.ShapeDtypeStruct((ROWS // HEADS, WIDE), bf16),
        in_specs=[anywhere] * 7,
        out_specs=pl.BlockSpec(memory_space=pltpu.VMEM),
        scratch_shapes=[
            pltpu.VMEM((ROWS, GROUP * HD), bf16),
            pltpu.VMEM((ROWS, HD), bf16),
            pltpu.VMEM((2, BLK), i32),
            pltpu.VMEM((3, 2 * CTX), i32),
            pltpu.VMEM((1, 2 * CTX), i32),
            pltpu.VMEM((GROUP * HD, WIDE), bf16),
            dma((7,)),
            pltpu.VMEM((2, CHIPS, PIECE, HD), bf16),
            pltpu.VMEM((GROUP * ROWS, 2 * HD), bf16),
            pltpu.VMEM((GROUP * ROWS, 2 * HD), f32),
            pltpu.VMEM((GROUP * ROWS, HD), f32),
            dma((2, CHIPS, 2)),
            dma((CHIPS, 5)),
            pltpu.VMEM((GROUP, ROWS, HD), bf16),
            pltpu.VMEM((2, 2, ROWS, HD), bf16),
            pltpu.VMEM((2, 2, ROWS, HD), bf16),
            pltpu.VMEM((2, 2, CHIPS, 16, HD), bf16),
            pltpu.VMEM((2, CHIPS, 16, HD), bf16),
            pltpu.VMEM((2, CHIPS, 16, HD), bf16),
            pltpu.VMEM((MIXED, MIXED), bf16),
            pltpu.VMEM((2, 2, ROWS, HD), bf16),
            dma((2, 2)),
            dma((2, 2)),
            dma((2, 2)),
            dma((2, 2)),
            pltpu.VMEM((2, HEADS, 2, TURN, HALF), bf16),
            pltpu.VMEM((2, 2, TURN, HALF), bf16),
            pltpu.VMEM((2, 2, 2, TURN, HALF), bf16),
            dma((2, 6)),
            dma((2, 6)),
        ],
        compiler_params=pltpu.CompilerParams(
            collective_id=0, has_side_effects=True, vmem_limit_bytes=48 << 20
        ),
        cost_estimate=pl.CostEstimate(
            flops=4 * GROUP * ROWS * ROWS * CTX * HD,
            bytes_accessed=GROUP * HD * WIDE * 2,
            transcendentals=GROUP * ROWS * ROWS * CTX,
        ),
        name="attend_and_project",
    )(
        queries, keys, values, segments.reshape(2, BLK), block_ranges.T, owner.reshape(1, 2 * CTX), out_proj
    )


def solution(mesh):
    return jax.shard_map(
        local,
        mesh=mesh,
        in_specs=(
            P("ctx", "head"),
            P("ctx", "head"),
            P("ctx", "head"),
            P("ctx"),
            P(),
            P(),
            P("head", None),
        ),
        out_specs=P(("ctx", "head"), None),
        check_vma=False,
    )
```

time: 172 us -> 108 us (0.63)
  waiting for transfers between devices: 40.4 us -> 0 us
  Pallas kernels: 76.6 us -> 100 us
  blocking collectives: 17.8 us -> 0 us
  between operations: 13.5 us -> 0.02 us
  starting transfers between devices: 8.62 us -> 0 us
  matrix products: 4.8 us -> 0 us
    reduce_scatter x1 -> x0, waiting for transfers between devices: 29.3 us -> none  [local(): return lax.psum_scatter(product, 'head', scatter_dimension=0, tiled=True)]
    pallas_call x1, Pallas kernels: 76.6 us -> 100 us  [local(): pl.pallas_call(kernel, out_shape=jax.ShapeDtypeStruct((ROWS // HEADS, WID...]
    all_to_all x1 -> x0, blocking collectives: 17.8 us -> none  [local(): lax.all_to_all(moved.reshape(CTX, 4, GROUP * HD), 'ctx', 0, 0, tiled=True)]
    all_to_all x1 -> x0, waiting for transfers between devices: 11 us -> none  [local(): lax.all_to_all(lead, 'ctx', 0, 0, tiled=True).reshape(CTX, 2, 2, GROUP * HD)]
    all_to_all x1 -> x0, starting transfers between devices: 8.58 us -> none  [local(): lax.all_to_all(lead, 'ctx', 0, 0, tiled=True).reshape(CTX, 2, 2, GROUP * HD)]
    dot_general x1 -> x0, matrix products: 4.8 us -> none  [local(): jnp.dot(owned, out_proj, preferred_element_type=jnp.float32)]
    unnamed x11 -> x15, local copies, waits for them, and re-layouts: 4.09 us -> 7.62 us
  transfers between devices with their start and end apart: 2 -> 0, of which waited for: 2 -> 0; matrix products, arithmetic and copies ran while one was open for 1% -> 0% of each run, Pallas kernels for 0% -> 0%
where the time goes in v2:
time: 108 us
  Pallas kernels  100 us (93%)
  local copies, waits for them, and re-layouts  7.62 us (7%)
    pallas_call x1, Pallas kernels, local(): pl.pallas_call(kernel, out_shape=jax.ShapeDtypeStruct((ROWS // HEADS, WID...  100 us
    unnamed x15, local copies, waits for them, and re-layouts  7.62 us

profile of v2, /device:TPU:1, one launch (start us, length us, event | category | flops | bytes accessed | tf_op | source)
XLA Modules:
  0.0 108.0 jit_solution(4665872252654735553)
XLA Ops:
  0.0 0.0 copy-start
  0.0 2.2 %copy-done = bf16[512,4096]{1,0:T(8,128)(2,1)S(1)} copy-done((bf16[512,4096]{1,0:T(8,128)(2,1)S(1)}, bf16[512,4096]{1,0:T(8,128)(2,1)}, u32[]{:S(2)}) %copy-start) | copy-done | bytes 4194328
  2.2 0.0 copy-start.1
  2.2 0.9 copy-done.1
  3.1 0.0 copy-start.2
  3.1 0.8 copy-done.2
  4.0 0.0 copy-start.3
  4.0 0.8 copy-done.3
  4.8 0.0 copy-start.4
  4.8 0.7 copy-done.4
  5.5 0.0 copy-start.5
  5.5 0.7 copy-done.5
  6.2 0.0 copy-start.6
  6.2 0.7 copy-done.6
  6.8 100.3 %attend_and_project.1 = bf16[64,4096]{1,0:T(8,128)(2,1)S(1)} custom-call(bf16[256,512]{1,0:T(8,128)(2,1)S(1)} %copy-done.1, bf16[256,128]{1,0:T(8,128)(2,1)S(1)} %copy-done.2, bf16[256,128]{1,0:T(8,128)(2,1)S(1)} %copy-done.3, s32[2,128]{1,0:T(2,128)S(1)} %bitcast.4, s32[3,128]{1,0:T(4,128)S(1)} %bitcast.3, s32[1,128]{1,0:T(1,128)S(1)} %bitcast.5, ...), custom_call_target="tpu_custom_call" | custom-call | flops 8589934592 | bytes 4194304 | tf_op jit(solution)/shard_map/attend_and_project/pallas_call | solution.py:497
  107.2 0.8 copy.9
Async XLA Ops:
  0.0 2.2 %copy-start = (bf16[512,4096]{1,0:T(8,128)(2,1)S(1)}, bf16[512,4096]{1,0:T(8,128)(2,1)}, u32[]{:S(2)}) copy-start(bf16[512,4096]{1,0:T(8,128)(2,1)} %proj_hbm.1) | copy-start | bytes 12582916
  2.2 0.9 copy-start.1
  3.1 0.8 copy-start.2
  4.0 0.8 copy-start.3
  4.8 0.7 copy-start.4
  5.5 0.7 copy-start.5
  6.2 0.7 copy-start.6

commit v3 on v2

--- a/solution.py
+++ b/solution.py
@@ -24,8 +24,8 @@
 TURN = 32
 MIXED = CHIPS * 16
 CLASSES = 16
-TRIPLE = 3
-LOOKAHEAD = 1
+BATCH = 4
+LOOKAHEAD = 3
 DOC_STEP = 32768
 MASKED = -1e30
 SCALE = math.log2(math.e) / math.sqrt(HD)
@@ -113,17 +113,10 @@
     barrier = pltpu.get_barrier_semaphore()
     sibling = place.device(place.chip(0, 0, other))
 
-    def greet(step, carry):
-        target = place.device(place.chip(step // NZ, step % NZ, core))
-        pl.semaphore_signal(barrier, inc=1, device_id=target, device_id_type=MESH)
-        return carry
-
-    lax.fori_loop(1, CHIPS, greet, 0)
-    pl.semaphore_signal(barrier, inc=1, device_id=sibling, device_id_type=MESH)
-    for step in (1, -1):
-        pl.semaphore_signal(
-            barrier, inc=1, device_id={"ctx": me, "head": place.plane(step)}, device_id_type=MESH
-        )
+    around = [place.device(place.chip(dx, dz, core)) for dx, dz in ((1, 0), (-1, 0), (0, 1), (0, -1))]
+    around += [sibling] + [{"ctx": me, "head": place.plane(step)} for step in (1, -1)]
+    for device in around:
+        pl.semaphore_signal(barrier, inc=1, device_id=device, device_id_type=MESH)
 
     for load in loads[:3]:
         load.wait()
@@ -134,7 +127,7 @@
     held[core, 0, ROWS:KSEG, :] = jnp.concatenate(
         [seg_rows, jnp.full((1, BLK), me, jnp.int32).astype(jnp.float32), jnp.zeros((13, BLK), jnp.float32)], axis=0
     ).astype(jnp.bfloat16)
-    pl.semaphore_wait(barrier, CHIPS - 1 + 1 + 2)
+    pl.semaphore_wait(barrier, len(around))
 
     parts = {"all": (0, PIECE, 0), "keys": (0, KSEG, 0), "values": (KSEG, ROWS, 1)}
 
@@ -280,12 +273,17 @@
             key_parts.append(jnp.concatenate(blocks, axis=1))
             value_parts.append(with_ones(held[role, index, KSEG:PIECE, :]))
         value_all = jnp.concatenate(value_parts, axis=0)
+        by_head = []
         for head in range(GROUP):
             rows = slice(head * ROWS, (head + 1) * ROWS)
             scores = []
             for key in key_parts:
                 score = exact(scaled[rows, 0 : HD + CLASSES], key)
                 scores += [score[:, 0:BLK], score[:, BLK : 2 * BLK]]
+            by_head.append(scores)
+        for head in range(GROUP):
+            rows = slice(head * ROWS, (head + 1) * ROWS)
+            scores = by_head[head]
             largest = functools.reduce(jnp.maximum, scores)
             old = top[rows, :]
             new = jnp.maximum(old, jnp.max(largest, axis=1, keepdims=True))
@@ -298,11 +296,9 @@
             total[rows, 0:HD] = total[rows, 0:HD] * factor + added[:, 0:HD]
             total[rows, HD : 2 * HD] = total[rows, HD : 2 * HD] * factor + added[:, HD : 2 * HD]
 
-    steps = (2 * CHIPS - 1) // TRIPLE
-    reached = [0]
-    for step in range(steps):
-        reached.append(min(CHIPS - 1, (TRIPLE * step + 3) // 2 + LOOKAHEAD))
-    reached[-1] = CHIPS - 1
+    start = (2 * CHIPS - 1) % BATCH
+    steps = (2 * CHIPS - 1) // BATCH
+    reached = [min(CHIPS - 1, (start + BATCH * step) // 2 + LOOKAHEAD) for step in range(steps)] + [CHIPS - 1]
 
     def events(step, low, high):
         if high - low == 1:
@@ -320,20 +316,22 @@
         def _():
             events(step, middle, high)
 
+    def take(at):
+        own = at % 2
+        role, index = (core + 1 + own) % 2, (at + own) // 2
+
+        @pl.when(own == 0)
+        def _():
+            copy((role, index), "all", 0, index, me).wait_recv()
+
+        return role, index
+
+    forward(tuple(range(1, reached[0] + 1)))
+    attend([take(jnp.int32(at)) for at in range(start)])
+
     def one_step(step, carry):
         events(step, 0, steps)
-        pieces = []
-        for each in range(TRIPLE):
-            at = TRIPLE * step + each
-            own = at % 2
-            role, index = (core + 1 + own) % 2, (at + own) // 2
-
-            @pl.when(own == 0)
-            def _(role=role, index=index):
-                copy((role, index), "all", 0, index, me).wait_recv()
-
-            pieces.append((role, index))
-        attend(pieces)
+        attend([take(start + BATCH * step + each) for each in range(BATCH)])
         return carry
 
     lax.fori_loop(0, steps, one_step, 0)
@@ -414,17 +412,19 @@
     def eights(rows):
         return rows.astype(jnp.float32).reshape(CHIPS, 8, HD)
 
-    for turn in range(2):
+    def deal(turn):
         swap(turn, 0).wait_recv()
         both = jnp.concatenate([eights(owned[turn, core]), eights(swap_in[0, turn])], axis=1)
         spread_out[0, turn] = both.astype(jnp.bfloat16)
         spread(turn, 0)
-    for turn in range(2):
+
+    def reorder(turn):
         spread_arrived(turn, 0)
         came_rows = spread_in[turn].reshape(MIXED, HD)
         spread_out[1, turn] = exact(mix[...], came_rows).astype(jnp.bfloat16).reshape(CHIPS, 16, HD)
         spread(turn, 1)
-    for turn in range(2):
+
+    def collect(turn):
         spread_arrived(turn, 1)
         landed = back_in[turn].astype(jnp.float32)
         owned[turn, core] = landed[:, 0:8, :].reshape(ROWS, HD).astype(jnp.bfloat16)
@@ -445,8 +445,7 @@
             device_id={"ctx": me, "head": place.plane(way)}, device_id_type=MESH,
         )
 
-    loads[6].wait()
-    for turn in range(2):
+    def project(turn):
         swap(turn, 1).wait_recv()
         owned[turn, other] = swap_in[1, turn]
         lefts = []
@@ -464,7 +463,7 @@
                     ]
         for message in range(4):
             give(turn, message).start()
-    for turn in range(2):
+    def relay(turn):
         for message in (4, 5):
             way = 1 if message == 4 else -1
             side = message - 4
@@ -473,7 +472,8 @@
             merged = part[turn, dest, side].astype(jnp.float32) + first_in[turn, side].astype(jnp.float32)
             part[turn, dest, side] = merged.astype(jnp.bfloat16)
             give(turn, message).start()
-    for turn in range(2):
+
+    def finish(turn):
         for message in range(2, 6):
             give(turn, message).wait_recv()
         for side in range(2):
@@ -482,6 +482,20 @@
                 summed = summed + last_in[turn, way, side].astype(jnp.float32)
             out[turn * TURN : (turn + 1) * TURN, side * HALF : (side + 1) * HALF] = summed.astype(jnp.bfloat16)
 
+    deal(0)
+    deal(1)
+    loads[6].wait()
+    reorder(0)
+    collect(0)
+    project(0)
+    reorder(1)
+    relay(0)
+    collect(1)
+    project(1)
+    relay(1)
+    finish(0)
+    finish(1)
+
     for turn in range(2):
         for way in range(2):
             swap(turn, way).wait_send()
@@ -491,7 +505,7 @@
 
 
 def local(queries, keys, values, segments, block_ranges, owner, out_proj):
-    anywhere = pl.BlockSpec(memory_space=pl.ANY)
+    anywhere = pl.BlockSpec(memory_space=pltpu.HBM)
     bf16, i32, f32 = jnp.bfloat16, jnp.int32, jnp.float32
     dma = pltpu.SemaphoreType.DMA
     return pl.pallas_call(
@@ -532,7 +546,7 @@
             dma((2, 6)),
         ],
         compiler_params=pltpu.CompilerParams(
-            collective_id=0, has_side_effects=True, vmem_limit_bytes=48 << 20
+            collective_id=0, has_side_effects=True, vmem_limit_bytes=60 << 20
         ),
         cost_estimate=pl.CostEstimate(
             flops=4 * GROUP * ROWS * ROWS * CTX * HD,

time: 108 us -> 92 us (0.85)
  Pallas kernels: 100 us -> 90 us
  local copies, waits for them, and re-layouts: 7.62 us -> 1.87 us
    pallas_call x1, Pallas kernels: 100 us -> 90 us  [local(): pl.pallas_call(kernel, out_shape=jax.ShapeDtypeStruct((ROWS // HEADS, WID...]
    unnamed x15 -> x1, local copies, waits for them, and re-layouts: 7.62 us -> 1.87 us
where the time goes in v3:
time: 92 us; the launch traced here: 91.9 us
  Pallas kernels  90 us (98%)
  local copies, waits for them, and re-layouts  1.87 us (2%)
    pallas_call x1, Pallas kernels, local(): pl.pallas_call(kernel, out_shape=jax.ShapeDtypeStruct((ROWS // HEADS, WID...  90 us
    unnamed x1, local copies, waits for them, and re-layouts  1.87 us

profile of v3, /device:TPU:1, one launch (start us, length us, event | category | flops | bytes accessed | tf_op | source)
XLA Modules:
  0.0 91.9 jit_solution(12350275253716539524)
XLA Ops:
  0.0 90.0 %attend_and_project.1 = bf16[64,4096]{1,0:T(8,128)(2,1)} custom-call(bf16[256,512]{1,0:T(8,128)(2,1)} %queries_hbm.1, bf16[256,128]{1,0:T(8,128)(2,1)} %keys_hbm.1, bf16[256,128]{1,0:T(8,128)(2,1)} %values_hbm.1, s32[2,128]{1,0:T(2,128)} %bitcast.4, s32[3,128]{1,0:T(4,128)} %bitcast.3, s32[1,128]{1,0:T(1,128)} %bitcast.5, bf16[512,4096]{1,0:T(8,128)(2,1)} %proj_hbm.1), custom_call_target="tpu_custom_call" | custom-call | flops 8589934592 | bytes 4194304 | tf_op jit(solution)/shard_map/attend_and_project/pallas_call | solution.py:511
  90.0 1.9 %copy.9 = bf16[64,4096]{1,0:T(8,128)(2,1)} copy(bf16[64,4096]{1,0:T(8,128)(2,1)} %attend_and_project.1) | data formatting | bytes 1048576

commit v4 on v3

--- a/solution.py
+++ b/solution.py
@@ -26,6 +26,7 @@
 CLASSES = 16
 BATCH = 4
 LOOKAHEAD = 3
+LAG = 5
 DOC_STEP = 32768
 MASKED = -1e30
 SCALE = math.log2(math.e) / math.sqrt(HD)
@@ -87,7 +88,7 @@
     queries_hbm, keys_hbm, values_hbm, segs_hbm, ranges_hbm, owner_hbm, proj_hbm, out,
     queries, keys, segs, ranges, owner, proj, load_sem,
     held, scaled, total, top, recv_sem, send_sem,
-    attn, swap_out, swap_in, spread_out, spread_in, back_in, mix, owned, swap_send, swap_recv, spread_send, spread_recv,
+    shuffle, swap_out, swap_in, spread_out, spread_in, back_in, mix, owned, swap_send, swap_recv, spread_send, spread_recv,
     part, first_in, last_in, sum_send, sum_recv,
 ):
     place = Place()
@@ -219,10 +220,20 @@
     ]
     row_class = jnp.concatenate([row_seg[0], row_seg[1] + 3], axis=0)
     chosen = one_hot(row_class[:, 0:CLASSES] == iota((ROWS, CLASSES), 1))
-    for head in range(GROUP):
-        rows = slice(head * ROWS, (head + 1) * ROWS)
-        scaled[rows, 0:HD] = queries[:, head * HD : (head + 1) * HD]
-        scaled[rows, HD : HD + CLASSES] = chosen
+    def by_turn(array, turn):
+        starts = [block * BLK + side * 2 * TURN + turn * TURN for block in range(2) for side in range(2)]
+        return jnp.concatenate([array[start : start + TURN, :] for start in starts], axis=0)
+
+    def rows_of(turn, head):
+        start = turn * GROUP * BLK + head * BLK
+        return slice(start, start + BLK)
+
+    all_queries = queries[...]
+    for turn in range(2):
+        turn_queries, turn_chosen = by_turn(all_queries, turn), by_turn(chosen, turn)
+        for head in range(GROUP):
+            scaled[rows_of(turn, head), 0:HD] = turn_queries[:, head * HD : (head + 1) * HD]
+            scaled[rows_of(turn, head), HD : HD + CLASSES] = turn_chosen
 
     def with_ones(value):
         return jnp.concatenate([value, jnp.ones_like(value)], axis=1)
@@ -247,10 +258,11 @@
             (wide >= jnp.concatenate([start, start], axis=1)) & (wide <= jnp.concatenate([end, end], axis=1))
         )
     hidden = jnp.where(jnp.concatenate(inside, axis=0), 0.0, MASKED)
-    for head in range(GROUP):
-        rows = slice(head * ROWS, (head + 1) * ROWS)
+    for part_at in range(GROUP):
+        rows = slice(part_at * ROWS, (part_at + 1) * ROWS)
+        turn_hidden = by_turn(hidden, part_at // 2)
         score = exact(scaled[rows, 0:HD], own_key)
-        score = jnp.where(hidden < 0.0, MASKED, score)
+        score = jnp.where(jnp.concatenate([turn_hidden, turn_hidden], axis=0) < 0.0, MASKED, score)
         new = jnp.broadcast_to(jnp.max(score, axis=1, keepdims=True), (ROWS, HD))
         top[rows, :] = new
         expo = jnp.concatenate(
@@ -259,31 +271,30 @@
         )
         total[rows, :] = exact(expo, own_value)
 
-    def attend(pieces):
-        key_parts, value_parts = [], []
-        for role, index in pieces:
-            blocks = []
-            for block, line in enumerate(line_of(role, index)):
-                spot = jnp.broadcast_to(line, (CLASSES, BLK))
-                seen = (spot >= class_from) & (spot <= class_to)
-                extra = jnp.where(seen, 0.0, MASKED).astype(jnp.bfloat16)
-                blocks.append(
-                    jnp.concatenate([held[role, index, block * BLK : (block + 1) * BLK, :], extra], axis=0)
-                )
-            key_parts.append(jnp.concatenate(blocks, axis=1))
-            value_parts.append(with_ones(held[role, index, KSEG:PIECE, :]))
-        value_all = jnp.concatenate(value_parts, axis=0)
-        by_head = []
-        for head in range(GROUP):
-            rows = slice(head * ROWS, (head + 1) * ROWS)
-            scores = []
-            for key in key_parts:
-                score = exact(scaled[rows, 0 : HD + CLASSES], key)
-                scores += [score[:, 0:BLK], score[:, BLK : 2 * BLK]]
-            by_head.append(scores)
-        for head in range(GROUP):
-            rows = slice(head * ROWS, (head + 1) * ROWS)
-            scores = by_head[head]
+    def attend(*work):
+        ready = []
+        for pieces, turns in work:
+            key_parts, value_parts = [], []
+            for role, index in pieces:
+                blocks = []
+                for block, line in enumerate(line_of(role, index)):
+                    spot = jnp.broadcast_to(line, (CLASSES, BLK))
+                    seen = (spot >= class_from) & (spot <= class_to)
+                    extra = jnp.where(seen, 0.0, MASKED).astype(jnp.bfloat16)
+                    blocks.append(
+                        jnp.concatenate([held[role, index, block * BLK : (block + 1) * BLK, :], extra], axis=0)
+                    )
+                key_parts.append(jnp.concatenate(blocks, axis=1))
+                value_parts.append(with_ones(held[role, index, KSEG:PIECE, :]))
+            value_all = jnp.concatenate(value_parts, axis=0)
+            for part_at in [2 * turn + half for turn in turns for half in range(2)]:
+                rows = slice(part_at * ROWS, (part_at + 1) * ROWS)
+                scores = []
+                for key in key_parts:
+                    score = exact(scaled[rows, 0 : HD + CLASSES], key)
+                    scores += [score[:, 0:BLK], score[:, BLK : 2 * BLK]]
+                ready.append((rows, scores, value_all))
+        for rows, scores, value_all in ready:
             largest = functools.reduce(jnp.maximum, scores)
             old = top[rows, :]
             new = jnp.maximum(old, jnp.max(largest, axis=1, keepdims=True))
@@ -296,105 +307,6 @@
             total[rows, 0:HD] = total[rows, 0:HD] * factor + added[:, 0:HD]
             total[rows, HD : 2 * HD] = total[rows, HD : 2 * HD] * factor + added[:, HD : 2 * HD]
 
-    start = (2 * CHIPS - 1) % BATCH
-    steps = (2 * CHIPS - 1) // BATCH
-    reached = [min(CHIPS - 1, (start + BATCH * step) // 2 + LOOKAHEAD) for step in range(steps)] + [CHIPS - 1]
-
-    def events(step, low, high):
-        if high - low == 1:
-            indices = tuple(range(reached[low] + 1, reached[low + 1] + 1))
-            if indices:
-                forward(indices)
-            return
-        middle = (low + high) // 2
-
-        @pl.when(step < middle)
-        def _():
-            events(step, low, middle)
-
-        @pl.when(step >= middle)
-        def _():
-            events(step, middle, high)
-
-    def take(at):
-        own = at % 2
-        role, index = (core + 1 + own) % 2, (at + own) // 2
-
-        @pl.when(own == 0)
-        def _():
-            copy((role, index), "all", 0, index, me).wait_recv()
-
-        return role, index
-
-    forward(tuple(range(1, reached[0] + 1)))
-    attend([take(jnp.int32(at)) for at in range(start)])
-
-    def one_step(step, carry):
-        events(step, 0, steps)
-        attend([take(start + BATCH * step + each) for each in range(BATCH)])
-        return carry
-
-    lax.fori_loop(0, steps, one_step, 0)
-
-    for role in range(2):
-
-        @pl.when(core == role)
-        def _(role=role):
-            for index in range(CHIPS):
-                for each in sends(role, index):
-                    each.wait_send()
-
-    for head in range(GROUP):
-        rows = slice(head * ROWS, (head + 1) * ROWS)
-        attn[head] = (total[rows, 0:HD] / total[rows, HD : 2 * HD]).astype(jnp.bfloat16)
-
-    at_out, at_in = iota((ROWS, ROWS), 0), iota((ROWS, ROWS), 1)
-    scatter_rows = one_hot(at_in == (at_out % 8) * TURN + at_out // 8)
-    gather_rows = one_hot(at_in == (at_out % TURN) * 8 + ((at_out % 64) // TURN) * GROUP + at_out // 64)
-
-    def swap(turn, way):
-        return pltpu.make_async_remote_copy(
-            src_ref=swap_out.at[way, turn], dst_ref=swap_in.at[way, turn],
-            send_sem=swap_send.at[way, turn], recv_sem=swap_recv.at[way, turn],
-            device_id=sibling, device_id_type=MESH,
-        )
-
-    def spread(turn, way):
-        target = spread_in if way == 0 else back_in
-
-        def one(step, carry):
-            there = ctx_of((place.x + step // NZ) % NX, (place.z + step % NZ) % NZ, core)
-            pltpu.make_async_remote_copy(
-                src_ref=spread_out.at[way, turn, there // CORES], dst_ref=target.at[turn, place.chip_here],
-                send_sem=spread_send.at[way, turn], recv_sem=spread_recv.at[way, turn],
-                device_id=place.device(there), device_id_type=MESH,
-            ).start()
-            return carry
-
-        lax.fori_loop(1, CHIPS, one, 0)
-        target[turn, place.chip_here] = spread_out[way, turn, place.chip_here]
-
-    def spread_arrived(turn, way):
-        target = spread_in if way == 0 else back_in
-        many = target.at[turn, pl.ds(0, CHIPS - 1)]
-        pltpu.make_async_copy(many, many, spread_recv.at[way, turn]).wait()
-
-    def spread_sent(turn, way):
-        many = spread_out.at[way, turn, pl.ds(0, CHIPS - 1)]
-        pltpu.make_async_copy(many, many, spread_send.at[way, turn]).wait()
-
-    for turn in range(2):
-        for block in range(2):
-            planes = [
-                attn[head, block * BLK + 64 * side + TURN * turn : block * BLK + 64 * side + TURN * (turn + 1), :]
-                for side in range(2)
-                for head in range(GROUP)
-            ]
-            dealt = exact(scatter_rows, jnp.concatenate(planes, axis=0)).astype(jnp.bfloat16)
-            owned[turn, block] = dealt
-        swap_out[0, turn] = owned[turn, other]
-        swap(turn, 0).start()
-
     def block_core(at):
         return jnp.where((at % 16) // 8 == 0, core, other)
 
@@ -408,6 +320,109 @@
     for at in range(MIXED // BLK):
         columns = slice(at * BLK, (at + 1) * BLK)
         mix[:, columns] = one_hot(code_out == jnp.broadcast_to(code_in[:, columns], (MIXED, BLK)))
+
+    at_out, at_in = iota((ROWS, ROWS), 0), iota((ROWS, ROWS), 1)
+    shuffle[0] = one_hot(at_in == (at_out % 8) * TURN + at_out // 8)
+    shuffle[1] = one_hot(at_in == (at_out % TURN) * 8 + ((at_out % 64) // TURN) * GROUP + at_out // 64)
+
+    start = (2 * CHIPS - 1) % BATCH
+    steps = (2 * CHIPS - 1) // BATCH
+    reached = [min(CHIPS - 1, (start + BATCH * step) // 2 + LOOKAHEAD) for step in range(steps)] + [CHIPS - 1]
+
+    def events(step, low, high):
+        if high - low == 1:
+            indices = tuple(range(reached[low] + 1, reached[low + 1] + 1))
+            if indices:
+                forward(indices)
+            return
+        middle = (low + high) // 2
+
+        @pl.when(step < middle)
+        def _():
+            events(step, low, middle)
+
+        @pl.when(step >= middle)
+        def _():
+            events(step, middle, high)
+
+    def used(at):
+        own = at % 2
+        return (core + 1 + own) % 2, (at + own) // 2
+
+    def take(at):
+        role, index = used(at)
+
+        @pl.when(at % 2 == 0)
+        def _():
+            copy((role, index), "all", 0, index, me).wait_recv()
+
+        return role, index
+
+    def batch(step, get):
+        return [get(start + BATCH * step + each) for each in range(BATCH)]
+
+    forward(tuple(range(1, reached[0] + 1)))
+    attend(([take(jnp.int32(at)) for at in range(start)], (0, 1)))
+
+    def first_half(step, carry):
+        events(step, 0, steps)
+        attend((batch(step, take), (0,)))
+        return carry
+
+    def both_halves(step, carry):
+        events(step, 0, steps)
+        attend((batch(step, take), (0,)), (batch(step - LAG, used), (1,)))
+        return carry
+
+    def second_half(step, carry):
+        attend((batch(step, used), (1,)))
+        return carry
+
+    lax.fori_loop(0, LAG, first_half, 0)
+    lax.fori_loop(LAG, steps, both_halves, 0)
+
+    def swap(turn, way):
+        return pltpu.make_async_remote_copy(
+            src_ref=swap_out.at[way, turn], dst_ref=swap_in.at[way, turn],
+            send_sem=swap_send.at[way, turn], recv_sem=swap_recv.at[way, turn],
+            device_id=sibling, device_id_type=MESH,
+        )
+
+    def spread(turn, way):
+        target = spread_in if way == 0 else back_in
+
+        def one(step, carry):
+            there = ctx_of((place.x + step // NZ) % NX, (place.z + step % NZ) % NZ, core)
+            pltpu.make_async_remote_copy(
+                src_ref=spread_out.at[way, turn, there // CORES], dst_ref=target.at[turn, place.chip_here],
+                send_sem=spread_send.at[way, turn], recv_sem=spread_recv.at[way, turn],
+                device_id=place.device(there), device_id_type=MESH,
+            ).start()
+            return carry
+
+        lax.fori_loop(1, CHIPS, one, 0)
+        target[turn, place.chip_here] = spread_out[way, turn, place.chip_here]
+
+    def spread_arrived(turn, way):
+        target = spread_in if way == 0 else back_in
+        many = target.at[turn, pl.ds(0, CHIPS - 1)]
+        pltpu.make_async_copy(many, many, spread_recv.at[way, turn]).wait()
+
+    def spread_sent(turn, way):
+        many = spread_out.at[way, turn, pl.ds(0, CHIPS - 1)]
+        pltpu.make_async_copy(many, many, spread_send.at[way, turn]).wait()
+
+    def close(turn):
+        done = [
+            (total[rows, 0:HD] / total[rows, HD : 2 * HD]).astype(jnp.bfloat16)
+            for rows in (rows_of(turn, head) for head in range(GROUP))
+        ]
+        for block in range(2):
+            starts = [block * 2 * TURN + side * TURN for side in range(2)]
+            planes = [done[head][start : start + TURN, :] for start in starts for head in range(GROUP)]
+            owned[turn, block] = exact(shuffle[0], jnp.concatenate(planes, axis=0)).astype(jnp.bfloat16)
+        swap_out[0, turn] = owned[turn, other]
+        swap(turn, 0).start()
 
     def eights(rows):
         return rows.astype(jnp.float32).reshape(CHIPS, 8, HD)
@@ -450,7 +465,7 @@
         owned[turn, other] = swap_in[1, turn]
         lefts = []
         for block in range(2):
-            sorted_rows = exact(gather_rows, owned[turn, block]).astype(jnp.bfloat16)
+            sorted_rows = exact(shuffle[1], owned[turn, block]).astype(jnp.bfloat16)
             lefts.append(jnp.concatenate([sorted_rows[64 * head : 64 * (head + 1), :] for head in range(GROUP)], axis=1))
         left = jnp.concatenate(lefts, axis=0)
         for side in range(2):
@@ -482,10 +497,15 @@
                 summed = summed + last_in[turn, way, side].astype(jnp.float32)
             out[turn * TURN : (turn + 1) * TURN, side * HALF : (side + 1) * HALF] = summed.astype(jnp.bfloat16)
 
+    middle = steps - LAG + 1
+    close(0)
+    lax.fori_loop(steps - LAG, middle, second_half, 0)
     deal(0)
+    lax.fori_loop(middle, steps, second_half, 0)
+    close(1)
+    reorder(0)
     deal(1)
     loads[6].wait()
-    reorder(0)
     collect(0)
     project(0)
     reorder(1)
@@ -494,6 +514,15 @@
     project(1)
     relay(1)
     finish(0)
+
+    for role in range(2):
+
+        @pl.when(core == role)
+        def _(role=role):
+            for index in range(CHIPS):
+                for each in sends(role, index):
+                    each.wait_send()
+
     finish(1)
 
     for turn in range(2):
@@ -527,7 +556,7 @@
             pltpu.VMEM((GROUP * ROWS, HD), f32),
             dma((2, CHIPS, 2)),
             dma((CHIPS, 5)),
-            pltpu.VMEM((GROUP, ROWS, HD), bf16),
+            pltpu.VMEM((2, ROWS, ROWS), bf16),
             pltpu.VMEM((2, 2, ROWS, HD), bf16),
             pltpu.VMEM((2, 2, ROWS, HD), bf16),
             pltpu.VMEM((2, 2, CHIPS, 16, HD), bf16),

time: 92 us -> 93.1 us (1.012)
  Pallas kernels: 90 us -> 91.1 us
    pallas_call x1, Pallas kernels: 90 us -> 91.1 us  [local(): pl.pallas_call(kernel, out_shape=jax.ShapeDtypeStruct((ROWS // HEADS, WID...]
where the time goes in v4:
time: 93.1 us; the launch traced here: 93 us
  Pallas kernels  91.1 us (98%)
  local copies, waits for them, and re-layouts  1.87 us (2%)
    pallas_call x1, Pallas kernels, local(): pl.pallas_call(kernel, out_shape=jax.ShapeDtypeStruct((ROWS // HEADS, WID...  91.1 us
    unnamed x1, local copies, waits for them, and re-layouts  1.87 us

profile of v4, /device:TPU:1, one launch (start us, length us, event | category | flops | bytes accessed | tf_op | source)
XLA Modules:
  0.0 93.0 jit_solution(769523320177028788)
XLA Ops:
  0.0 91.1 %attend_and_project.1 = bf16[64,4096]{1,0:T(8,128)(2,1)} custom-call(bf16[256,512]{1,0:T(8,128)(2,1)} %queries_hbm.1, bf16[256,128]{1,0:T(8,128)(2,1)} %keys_hbm.1, bf16[256,128]{1,0:T(8,128)(2,1)} %values_hbm.1, s32[2,128]{1,0:T(2,128)} %bitcast.4, s32[3,128]{1,0:T(4,128)} %bitcast.3, s32[1,128]{1,0:T(1,128)} %bitcast.5, bf16[512,4096]{1,0:T(8,128)(2,1)} %proj_hbm.1), custom_call_target="tpu_custom_call" | custom-call | flops 8589934592 | bytes 4194304 | tf_op jit(solution)/shard_map/attend_and_project/pallas_call | solution.py:540
  91.1 1.9 %copy.9 = bf16[64,4096]{1,0:T(8,128)(2,1)} copy(bf16[64,4096]{1,0:T(8,128)(2,1)} %attend_and_project.1) | data formatting | bytes 1048576

commit v5 on v4

v5 whole, which is shorter than its diff:
```python
import functools
import math

import jax
import jax.numpy as jnp
from jax import lax
from jax.experimental import pallas as pl
from jax.experimental.pallas import tpu as pltpu
from jax.sharding import PartitionSpec as P

MESH = pl.DeviceIdType.MESH
HD = 128
BLK = 128
GROUP = 4
NX, NZ, CORES = 4, 8, 2
CTX = NX * NZ * CORES
HEADS = 4
ROWS = 256
KSEG = ROWS + 16
PIECE = KSEG + ROWS
CHIPS = NX * NZ
WIDE = 4096
HALF = WIDE // 2
TURN = 32
MIXED = CHIPS * 16
BIAS = -(2**31)
LOOKAHEAD = 3
EARLY = 13
LAG = 8
MASKED = -1e30
SCALE = math.log2(math.e) / math.sqrt(HD)


def ctx_of(x, z, core):
    return (x * NZ + z) * CORES + core


def ring_offsets(size):
    half = size // 2
    found = [0]
    for step in range(1, half):
        found += [step, -step]
    return found + [half]


def piece_order(size_a, size_b):
    pieces = [(da, db) for da in ring_offsets(size_a) for db in ring_offsets(size_b)]
    return sorted(pieces, key=lambda piece: abs(piece[0]) + abs(piece[1]))


ORDERS = (piece_order(NX, NZ), piece_order(NZ, NX))


class Place:
    def __init__(self):
        ctx = lax.axis_index("ctx")
        self.ctx = ctx
        self.head = lax.axis_index("head")
        self.core = ctx % CORES
        self.z = (ctx // CORES) % NZ
        self.x = ctx // (CORES * NZ)
        self.chip_here = ctx // CORES

    def chip(self, dx, dz, core):
        return ctx_of((self.x + dx + NX) % NX, (self.z + dz + NZ) % NZ, core)

    def device(self, ctx):
        return {"ctx": ctx, "head": self.head}

    def plane(self, step):
        return (self.head + step) % HEADS


def iota(shape, dim):
    return lax.broadcasted_iota(jnp.int32, shape, dim)


def one_hot(mask):
    return jnp.where(mask, 1.0, 0.0).astype(jnp.bfloat16)


def exact(left, right):
    return jnp.dot(left, right, preferred_element_type=jnp.float32)


def kernel(
    queries_hbm, keys_hbm, values_hbm, segs_hbm, ranges_hbm, owner_hbm, proj_hbm, out,
    queries, keys, segs, ranges, owner, proj, load_sem,
    held, scaled, total, top, first, width, recv_sem, send_sem,
    shuffle, swap_out, swap_in, spread_out, spread_in, back_in, mix, owned, swap_send, swap_recv, spread_send, spread_recv,
    part, first_in, last_in, sum_send, sum_recv,
):
    place = Place()
    me, core, other = place.ctx, place.core, 1 - place.core

    loads = [
        pltpu.make_async_copy(source, target, load_sem.at[at])
        for at, (source, target) in enumerate(
            (
                (keys_hbm, keys),
                (segs_hbm, segs),
                (values_hbm, held.at[core, 0, pl.ds(KSEG, ROWS), :]),
                (queries_hbm, queries),
                (ranges_hbm, ranges),
                (owner_hbm, owner),
                (proj_hbm, proj),
            )
        )
    ]
    for load in loads:
        load.start()

    barrier = pltpu.get_barrier_semaphore()
    sibling = place.device(place.chip(0, 0, other))

    def greet(step, carry):
        target = place.device(place.chip(step // NZ, step % NZ, core))
        pl.semaphore_signal(barrier, inc=1, device_id=target, device_id_type=MESH)
        return carry

    lax.fori_loop(1, CHIPS, greet, 0)
    around = [sibling] + [{"ctx": me, "head": place.plane(step)} for step in (1, -1)]
    for device in around:
        pl.semaphore_signal(barrier, inc=1, device_id=device, device_id_type=MESH)

    for load in loads[:3]:
        load.wait()
    for block in range(2):
        turned = jnp.transpose(keys[block * BLK : (block + 1) * BLK, :].astype(jnp.float32))
        held[core, 0, block * BLK : (block + 1) * BLK, :] = turned.astype(jnp.bfloat16)
    seg_rows = segs[...].astype(jnp.float32)
    held[core, 0, ROWS:KSEG, :] = jnp.concatenate(
        [seg_rows, jnp.full((1, BLK), me, jnp.int32).astype(jnp.float32), jnp.zeros((13, BLK), jnp.float32)], axis=0
    ).astype(jnp.bfloat16)
    pl.semaphore_wait(barrier, CHIPS - 1 + len(around))

    parts = {"all": (0, PIECE, 0), "keys": (0, KSEG, 0), "values": (KSEG, ROWS, 1)}

    def copy(piece, name, kind, at, device):
        role, index = piece
        start, size, which = parts[name]
        return pltpu.make_async_remote_copy(
            src_ref=held.at[role, index, pl.ds(start, size), :],
            dst_ref=held.at[role, at, pl.ds(start, size), :],
            send_sem=send_sem.at[index, kind], recv_sem=recv_sem.at[role, at, which],
            device_id=place.device(device), device_id_type=MESH,
        )

    def sends(role, index):
        order = ORDERS[role]
        sizes = (NX, NZ) if role == 0 else (NZ, NX)
        offsets = order[index]
        found = []

        def go(name, axis, way):
            moved = list(offsets)
            moved[axis] -= way
            for each in range(2):
                if moved[each] <= -sizes[each] // 2:
                    moved[each] += sizes[each]
            step = [0, 0]
            step[axis] = way
            dx, dz = step if role == 0 else step[::-1]
            kind = 2 * axis + (0 if way > 0 else 1)
            found.append(copy((role, index), name, kind, order.index(tuple(moved)), place.chip(dx, dz, role)))

        for axis in range(2):
            if axis == 0 and offsets[1] != 0:
                continue
            offset, half = offsets[axis], sizes[axis] // 2
            if offset == 0:
                go("all", axis, 1)
                go("all", axis, -1)
            elif abs(offset) < half:
                name = "all" if abs(offset) < half - 1 else ("keys" if offset > 0 else "values")
                go(name, axis, -1 if offset > 0 else 1)
        found.append(copy((role, index), "all", 4, index, place.chip(0, 0, 1 - role)))
        return found

    def arrive(role, index):
        da, db = ORDERS[role][index]
        sizes = (NX, NZ) if role == 0 else (NZ, NX)
        if index == 0:
            return
        halves = db == sizes[1] // 2 or (db == 0 and da == sizes[0] // 2)
        for name in ("keys", "values") if halves else ("all",):
            copy((role, index), name, 0, index, me).wait_recv()

    def forward(indices):
        for role in range(2):

            @pl.when(core == role)
            def _(role=role):
                for index in indices:
                    arrive(role, index)
                    for each in sends(role, index):
                        each.start()

    forward((0,))

    for load in loads[3:6]:
        load.wait()

    def block_core(at):
        return jnp.where((at % 16) // 8 == 0, core, other)

    came = iota((BLK, MIXED), 1)
    expand = one_hot(iota((BLK, MIXED), 0) == 2 * (2 * (came // 16) + block_core(came)) + core)
    owner_rows = jnp.broadcast_to(owner[...].astype(jnp.float32), (8, BLK)).astype(jnp.bfloat16)
    owner_of = exact(owner_rows, expand)[0:1, :].astype(jnp.int32)
    code_in = owner_of * 8 + iota((1, MIXED), 1) % 8
    leaves = iota((MIXED, BLK), 0)
    code_out = (2 * (leaves // 16) + block_core(leaves)) * 8 + leaves % 8
    for at in range(MIXED // BLK):
        columns = slice(at * BLK, (at + 1) * BLK)
        mix[:, columns] = one_hot(code_out == jnp.broadcast_to(code_in[:, columns], (MIXED, BLK)))

    at_out, at_in = iota((ROWS, ROWS), 0), iota((ROWS, ROWS), 1)
    shuffle[0] = one_hot(at_in == (at_out % 8) * TURN + at_out // 8)
    shuffle[1] = one_hot(at_in == (at_out % TURN) * 8 + ((at_out % 64) // TURN) * GROUP + at_out // 64)

    def swap(turn, way):
        return pltpu.make_async_remote_copy(
            src_ref=swap_out.at[way, turn], dst_ref=swap_in.at[way, turn],
            send_sem=swap_send.at[way, turn], recv_sem=swap_recv.at[way, turn],
            device_id=sibling, device_id_type=MESH,
        )

    def height(turn, way):
        return 32 if turn == 0 and way == 0 else 16

    def spread(turn, way):
        target = spread_in if way == 0 else back_in
        tall = height(turn, way)

        def one(step, carry):
            there = ctx_of((place.x + step // NZ) % NX, (place.z + step % NZ) % NZ, core)
            pltpu.make_async_remote_copy(
                src_ref=spread_out.at[way, turn, there // CORES, pl.ds(0, tall)],
                dst_ref=target.at[turn, place.chip_here, pl.ds(0, tall)],
                send_sem=spread_send.at[way, turn], recv_sem=spread_recv.at[way, turn],
                device_id=place.device(there), device_id_type=MESH,
            ).start()
            return carry

        lax.fori_loop(1, CHIPS, one, 0)
        target[turn, place.chip_here] = spread_out[way, turn, place.chip_here]

    def spread_arrived(turn, way):
        target = spread_in if way == 0 else back_in
        many = target.at[turn, pl.ds(0, CHIPS - 1), pl.ds(0, height(turn, way))]
        pltpu.make_async_copy(many, many, spread_recv.at[way, turn]).wait()

    def spread_sent(turn, way):
        many = spread_out.at[way, turn, pl.ds(0, CHIPS - 1), pl.ds(0, height(turn, way))]
        pltpu.make_async_copy(many, many, spread_send.at[way, turn]).wait()

    def close(turn):
        for block in range(2):
            starts = [block * BLK + side * 2 * TURN + turn * TURN for side in range(2)]
            planes = [
                queries[start : start + TURN, head * HD : (head + 1) * HD] for start in starts for head in range(GROUP)
            ]
            owned[turn, block] = exact(shuffle[0], jnp.concatenate(planes, axis=0)).astype(jnp.bfloat16)
        swap_out[0, turn, 0:ROWS, :] = owned[turn, other]
        swap_out[0, turn, ROWS:KSEG, :] = held[core, 0, ROWS:KSEG, :]
        swap(turn, 0).start()

    def eights(rows):
        return rows.astype(jnp.float32).reshape(CHIPS, 8, HD)

    def deal(turn):
        swap(turn, 0).wait_recv()
        both = jnp.concatenate([eights(owned[turn, core]), eights(swap_in[0, turn, 0:ROWS, :])], axis=1)
        spread_out[0, turn, :, 0:16, :] = both.astype(jnp.bfloat16)
        if turn == 0:
            theirs = swap_in[0, turn, ROWS:KSEG, :].astype(jnp.float32)
            docs = jnp.concatenate([seg_rows, theirs[0:2, :], jnp.zeros((12, BLK), jnp.float32)], axis=0)
            spread_out[0, turn, :, 16:32, :] = jnp.broadcast_to(docs.astype(jnp.bfloat16)[None], (CHIPS, 16, BLK))
        spread(turn, 0)

    def reorder(turn):
        spread_arrived(turn, 0)
        came_rows = spread_in[turn, :, 0:16, :].reshape(MIXED, HD)
        spread_out[1, turn, :, 0:16, :] = exact(mix[...], came_rows).astype(jnp.bfloat16).reshape(CHIPS, 16, HD)
        spread(turn, 1)

    def collect(turn):
        spread_arrived(turn, 1)
        landed = back_in[turn, :, 0:16, :].astype(jnp.float32)
        owned[turn, core] = landed[:, 0:8, :].reshape(ROWS, HD).astype(jnp.bfloat16)
        swap_out[1, turn, 0:ROWS, :] = landed[:, 8:16, :].reshape(ROWS, HD).astype(jnp.bfloat16)
        swap(turn, 1).start()

    def rows_of(turn, head):
        start = turn * GROUP * BLK + head * BLK
        return slice(start, start + BLK)

    def settle(turn):
        swap(turn, 1).wait_recv()
        owned[turn, other] = swap_in[1, turn, 0:ROWS, :]
        turned = [exact(shuffle[1], owned[turn, block]).astype(jnp.bfloat16) for block in range(2)]
        for head in range(GROUP):
            scaled[rows_of(turn, head), :] = jnp.concatenate(
                [turned[block][64 * head : 64 * (head + 1), :] for block in range(2)], axis=0
            )

    def intervals():
        docs = spread_in[0, :, 16:32, :].astype(jnp.float32)
        real = iota((16, BLK), 0) < 4
        begins = []
        for doc in (1.0, 2.0):
            before = jnp.sum(jnp.where(docs < doc, 1.0, 0.0), axis=0)
            before = jnp.sum(jnp.where(real, before, 0.0), axis=0, keepdims=True)
            begins.append(jnp.sum(before, axis=1, keepdims=True).astype(jnp.int32))
        one, two = (jnp.broadcast_to(begin, (64, BLK)) for begin in begins)
        lane = iota((1, BLK), 1)
        for block in range(2):
            mine = (owner[...] == me) & (lane % 2 == block)

            def pick(array):
                chosen = jnp.where(mine, array, 0).astype(jnp.float32)
                chosen = jnp.sum(chosen, axis=1, keepdims=True).astype(jnp.int32)
                return jnp.broadcast_to(chosen, (64, BLK))

            wanted = pick(lane)
            low, high, causal = (pick(ranges[at : at + 1, :]) for at in range(3))
            for turn in range(2):
                at = iota((64, BLK), 0)
                pos = wanted * BLK + (at // TURN) * 2 * TURN + turn * TURN + at % TURN
                start = jnp.maximum(low * BLK, jnp.where(pos >= two, two, jnp.where(pos >= one, one, 0)))
                end = jnp.where(pos < one, one, jnp.where(pos < two, two, CTX * ROWS)) - 1
                end = jnp.minimum(end, high * BLK + (BLK - 1))
                end = jnp.where(causal == 0, end, jnp.minimum(end, pos))
                first[turn, block * 64 : (block + 1) * 64, :] = jnp.int32(BIAS) - start
                width[turn, block * 64 : (block + 1) * 64, :] = (end - start + 1) + jnp.int32(BIAS)

    def with_ones(value):
        return jnp.concatenate([value, jnp.ones_like(value)], axis=1)

    def attend(*work):
        ready = []
        lane = iota((1, BLK), 1)
        for pieces, turns in work:
            key_parts, value_parts, lines = [], [], []
            for role, index in pieces:
                key_parts.append(
                    jnp.concatenate([held[role, index, 0:BLK, :], held[role, index, BLK : 2 * BLK, :]], axis=1)
                )
                value_parts.append(with_ones(held[role, index, KSEG:PIECE, :]))
                info = held[role, index, ROWS:KSEG, :].astype(jnp.float32).astype(jnp.int32)
                lines += [info[2:3, :] * ROWS + lane + block * BLK for block in range(2)]
            value_all = jnp.concatenate(value_parts, axis=0)
            for turn in turns:
                inside = [line + first[turn] < width[turn] for line in lines]
                for part_at in (2 * turn, 2 * turn + 1):
                    rows = slice(part_at * ROWS, (part_at + 1) * ROWS)
                    scores = []
                    for at, key in enumerate(key_parts):
                        score = exact(scaled[rows, :], key)
                        for block in range(2):
                            columns = slice(block * BLK, (block + 1) * BLK)
                            scores.append(
                                jnp.concatenate(
                                    [
                                        jnp.where(inside[2 * at + block], score[half : half + BLK, columns], MASKED)
                                        for half in (0, BLK)
                                    ],
                                    axis=0,
                                )
                            )
                    ready.append((rows, scores, value_all))
        for rows, scores, value_all in ready:
            largest = functools.reduce(jnp.maximum, scores)
            old = top[rows, :]
            new = jnp.maximum(old, jnp.max(largest, axis=1, keepdims=True))
            top[rows, :] = new
            factor = jnp.exp2((old - new) * SCALE)
            expo = jnp.concatenate(
                [jnp.exp2((score - new) * SCALE).astype(jnp.bfloat16) for score in scores], axis=1
            )
            added = exact(expo, value_all)
            total[rows, 0:HD] = total[rows, 0:HD] * factor + added[:, 0:HD]
            total[rows, HD : 2 * HD] = total[rows, HD : 2 * HD] * factor + added[:, HD : 2 * HD]

    steps = CHIPS // 2
    reached = [min(CHIPS - 1, max(EARLY, 2 * step + 1 + LOOKAHEAD)) for step in range(steps)]

    def events(step, low, high):
        if high - low == 1:
            indices = tuple(range((reached[low - 1] if low else EARLY) + 1, reached[low] + 1))
            if indices:
                forward(indices)
            return
        middle = (low + high) // 2

        @pl.when(step < middle)
        def _():
            events(step, low, middle)

        @pl.when(step >= middle)
        def _():
            events(step, middle, high)

    def used(step):
        return [(role, 2 * step + each) for role in (core, other) for each in range(2)]

    def take(step):
        pieces = used(step)
        for role, index in pieces[2:]:
            copy((role, index), "all", 0, index, me).wait_recv()
        return pieces

    def first_half(step, carry):
        events(step, 0, steps)
        attend((take(step), (0,)))
        return carry

    def both_halves(step, carry):
        events(step, 0, steps)
        attend((take(step), (0,)), (used(step - LAG), (1,)))
        return carry

    def second_half(step, carry):
        attend((used(step), (1,)))
        return carry

    def give(turn, message):
        way = 1 if message % 2 == 0 else -1
        side = (0, 1, 1, 0, 0, 1)[message]
        dest = place.plane(2 if message < 2 else way)
        if message < 2:
            target = first_in.at[turn, message]
        else:
            target = last_in.at[turn, message % 2, side]
        return pltpu.make_async_remote_copy(
            src_ref=part.at[turn, dest, side], dst_ref=target,
            send_sem=sum_send.at[turn, message], recv_sem=sum_recv.at[turn, message],
            device_id={"ctx": me, "head": place.plane(way)}, device_id_type=MESH,
        )

    def project(turn):
        left = jnp.concatenate(
            [
                (total[rows, 0:HD] / total[rows, HD : 2 * HD]).astype(jnp.bfloat16)
                for rows in (rows_of(turn, head) for head in range(GROUP))
            ],
            axis=1,
        )
        for side in range(2):
            for at in range(2):
                start = side * HALF + at * (HALF // 2)
                product = exact(left, proj[:, start : start + HALF // 2]).astype(jnp.bfloat16)
                for dest in range(HEADS):
                    part[turn, dest, side, :, at * (HALF // 2) : (at + 1) * (HALF // 2)] = product[
                        dest * TURN : (dest + 1) * TURN, :
                    ]
        for message in range(4):
            give(turn, message).start()
    def relay(turn):
        for message in (4, 5):
            way = 1 if message == 4 else -1
            side = message - 4
            give(turn, message - 4).wait_recv()
            dest = place.plane(way)
            merged = part[turn, dest, side].astype(jnp.float32) + first_in[turn, side].astype(jnp.float32)
            part[turn, dest, side] = merged.astype(jnp.bfloat16)
            give(turn, message).start()

    def finish(turn):
        for message in range(2, 6):
            give(turn, message).wait_recv()
        for side in range(2):
            summed = part[turn, place.head, side].astype(jnp.float32)
            for way in range(2):
                summed = summed + last_in[turn, way, side].astype(jnp.float32)
            out[turn * TURN : (turn + 1) * TURN, side * HALF : (side + 1) * HALF] = summed.astype(jnp.bfloat16)

    middle = steps - LAG + 1
    top[...] = jnp.full(top.shape, MASKED, jnp.float32)
    total[...] = jnp.zeros(total.shape, jnp.float32)
    close(0)
    close(1)
    deal(0)
    deal(1)
    forward(range(1, 5))
    reorder(0)
    reorder(1)
    forward(range(5, 12))
    intervals()
    collect(0)
    collect(1)
    forward(range(12, EARLY + 1))
    settle(0)
    settle(1)

    lax.fori_loop(0, LAG, first_half, 0)
    lax.fori_loop(LAG, steps, both_halves, 0)
    loads[6].wait()
    project(0)
    middle = steps - LAG + (LAG + 1) // 2
    lax.fori_loop(steps - LAG, middle, second_half, 0)
    relay(0)
    lax.fori_loop(middle, steps, second_half, 0)
    project(1)
    relay(1)
    finish(0)

    for role in range(2):

        @pl.when(core == role)
        def _(role=role):
            for index in range(CHIPS):
                for each in sends(role, index):
                    each.wait_send()

    finish(1)

    for turn in range(2):
        for way in range(2):
            swap(turn, way).wait_send()
            spread_sent(turn, way)
        for message in range(6):
            give(turn, message).wait_send()


def local(queries, keys, values, segments, block_ranges, owner, out_proj):
    anywhere = pl.BlockSpec(memory_space=pltpu.HBM)
    bf16, i32, f32 = jnp.bfloat16, jnp.int32, jnp.float32
    dma = pltpu.SemaphoreType.DMA
    return pl.pallas_call(
        kernel,
        out_shape=jax.ShapeDtypeStruct((ROWS // HEADS, WIDE), bf16),
        in_specs=[anywhere] * 7,
        out_specs=pl.BlockSpec(memory_space=pltpu.VMEM),
        scratch_shapes=[
            pltpu.VMEM((ROWS, GROUP * HD), bf16),
            pltpu.VMEM((ROWS, HD), bf16),
            pltpu.VMEM((2, BLK), i32),
            pltpu.VMEM((3, 2 * CTX), i32),
            pltpu.VMEM((1, 2 * CTX), i32),
            pltpu.VMEM((GROUP * HD, WIDE), bf16),
            dma((7,)),
            pltpu.VMEM((2, CHIPS, PIECE, HD), bf16),
            pltpu.VMEM((GROUP * ROWS, HD), bf16),
            pltpu.VMEM((GROUP * ROWS, 2 * HD), f32),
            pltpu.VMEM((GROUP * ROWS, HD), f32),
            pltpu.VMEM((2, BLK, BLK), i32),
            pltpu.VMEM((2, BLK, BLK), i32),
            dma((2, CHIPS, 2)),
            dma((CHIPS, 5)),
            pltpu.VMEM((2, ROWS, ROWS), bf16),
            pltpu.VMEM((2, 2, KSEG, HD), bf16),
            pltpu.VMEM((2, 2, KSEG, HD), bf16),
            pltpu.VMEM((2, 2, CHIPS, 32, HD), bf16),
            pltpu.VMEM((2, CHIPS, 32, HD), bf16),
            pltpu.VMEM((2, CHIPS, 32, HD), bf16),
            pltpu.VMEM((MIXED, MIXED), bf16),
            pltpu.VMEM((2, 2, ROWS, HD), bf16),
            dma((2, 2)),
            dma((2, 2)),
            dma((2, 2)),
            dma((2, 2)),
            pltpu.VMEM((2, HEADS, 2, TURN, HALF), bf16),
            pltpu.VMEM((2, 2, TURN, HALF), bf16),
            pltpu.VMEM((2, 2, 2, TURN, HALF), bf16),
            dma((2, 6)),
            dma((2, 6)),
        ],
        compiler_params=pltpu.CompilerParams(
            collective_id=0, has_side_effects=True, vmem_limit_bytes=60 << 20
        ),
        cost_estimate=pl.CostEstimate(
            flops=4 * GROUP * ROWS * ROWS * CTX * HD,
            bytes_accessed=GROUP * HD * WIDE * 2,
            transcendentals=GROUP * ROWS * ROWS * CTX,
        ),
        name="attend_and_project",
    )(
        queries, keys, values, segments.reshape(2, BLK), block_ranges.T, owner.reshape(1, 2 * CTX), out_proj
    )


def solution(mesh):
    return jax.shard_map(
        local,
        mesh=mesh,
        in_specs=(
            P("ctx", "head"),
            P("ctx", "head"),
            P("ctx", "head"),
            P("ctx"),
            P(),
            P(),
            P("head", None),
        ),
        out_specs=P(("ctx", "head"), None),
        check_vma=False,
    )
```

time: 93.1 us -> 92.8 us (level)
  Pallas kernels: 91.1 us -> 90 us
    pallas_call x1, Pallas kernels: 91.1 us -> 90 us  [local(): pl.pallas_call(kernel, out_shape=jax.ShapeDtypeStruct((ROWS // HEADS, WID...]
where the time goes in v5:
time: 92.8 us; the launch traced here: 91.9 us
  Pallas kernels  90 us (97%)
  local copies, waits for them, and re-layouts  1.87 us (2%)
    pallas_call x1, Pallas kernels, local(): pl.pallas_call(kernel, out_shape=jax.ShapeDtypeStruct((ROWS // HEADS, WID...  90 us
    unnamed x1, local copies, waits for them, and re-layouts  1.87 us

profile of v5, /device:TPU:1, one launch (start us, length us, event | category | flops | bytes accessed | tf_op | source)
XLA Modules:
  0.0 91.9 jit_solution(7014383864378715632)
XLA Ops:
  0.0 90.0 %attend_and_project.1 = bf16[64,4096]{1,0:T(8,128)(2,1)} custom-call(bf16[256,512]{1,0:T(8,128)(2,1)} %queries_hbm.1, bf16[256,128]{1,0:T(8,128)(2,1)} %keys_hbm.1, bf16[256,128]{1,0:T(8,128)(2,1)} %values_hbm.1, s32[2,128]{1,0:T(2,128)} %bitcast.4, s32[3,128]{1,0:T(4,128)} %bitcast.3, s32[1,128]{1,0:T(1,128)} %bitcast.5, bf16[512,4096]{1,0:T(8,128)(2,1)} %proj_hbm.1), custom_call_target="tpu_custom_call" | custom-call | flops 8589934592 | bytes 4194304 | tf_op jit(solution)/shard_map/attend_and_project/pallas_call | solution.py:531
  90.0 1.9 %copy.9 = bf16[64,4096]{1,0:T(8,128)(2,1)} copy(bf16[64,4096]{1,0:T(8,128)(2,1)} %attend_and_project.1) | data formatting | bytes 1048576

commit v6 on v4

--- a/solution.py
+++ b/solution.py
@@ -26,7 +26,6 @@
 CLASSES = 16
 BATCH = 4
 LOOKAHEAD = 3
-LAG = 5
 DOC_STEP = 32768
 MASKED = -1e30
 SCALE = math.log2(math.e) / math.sqrt(HD)
@@ -46,7 +45,8 @@
 
 def piece_order(size_a, size_b):
     pieces = [(da, db) for da in ring_offsets(size_a) for db in ring_offsets(size_b)]
-    return sorted(pieces, key=lambda piece: abs(piece[0]) + abs(piece[1]))
+    weights = [2 if size == NX else 3 for size in (size_a, size_b)]
+    return sorted(pieces, key=lambda piece: weights[0] * abs(piece[0]) + weights[1] * abs(piece[1]))
 
 
 ORDERS = (piece_order(NX, NZ), piece_order(NZ, NX))
@@ -142,6 +142,13 @@
             device_id=place.device(device), device_id_type=MESH,
         )
 
+    def pair_copy(role, index):
+        pair = held.at[role, pl.ds(index, 2)]
+        return pltpu.make_async_remote_copy(
+            src_ref=pair, dst_ref=pair, send_sem=send_sem.at[index, 4], recv_sem=recv_sem.at[role, index, 0],
+            device_id=sibling, device_id_type=MESH,
+        )
+
     def sends(role, index):
         order = ORDERS[role]
         sizes = (NX, NZ) if role == 0 else (NZ, NX)
@@ -170,7 +177,10 @@
             elif abs(offset) < half:
                 name = "all" if abs(offset) < half - 1 else ("keys" if offset > 0 else "values")
                 go(name, axis, -1 if offset > 0 else 1)
-        found.append(copy((role, index), "all", 4, index, place.chip(0, 0, 1 - role)))
+        if index in (0, CHIPS - 1):
+            found.append(copy((role, index), "all", 4, index, place.chip(0, 0, 1 - role)))
+        elif index % 2 == 0:
+            found.append(pair_copy(role, index - 1))
         return found
 
     def arrive(role, index):
@@ -349,37 +359,33 @@
         own = at % 2
         return (core + 1 + own) % 2, (at + own) // 2
 
-    def take(at):
-        role, index = used(at)
-
-        @pl.when(at % 2 == 0)
-        def _():
-            copy((role, index), "all", 0, index, me).wait_recv()
-
-        return role, index
-
     def batch(step, get):
         return [get(start + BATCH * step + each) for each in range(BATCH)]
 
+    def take(step):
+        last = 2 * step + 3
+
+        @pl.when(step < steps - 1)
+        def _():
+            pair_copy(other, last).wait_recv()
+
+        @pl.when(step == steps - 1)
+        def _():
+            copy((other, CHIPS - 1), "all", 0, CHIPS - 1, me).wait_recv()
+
+        return batch(step, used)
+
     forward(tuple(range(1, reached[0] + 1)))
-    attend(([take(jnp.int32(at)) for at in range(start)], (0, 1)))
-
-    def first_half(step, carry):
-        events(step, 0, steps)
-        attend((batch(step, take), (0,)))
-        return carry
+    copy((other, 0), "all", 0, 0, me).wait_recv()
+    pair_copy(other, 1).wait_recv()
+    attend(([used(jnp.int32(at)) for at in range(start)], (0, 1)))
 
     def both_halves(step, carry):
         events(step, 0, steps)
-        attend((batch(step, take), (0,)), (batch(step - LAG, used), (1,)))
+        attend((take(step), (0, 1)))
         return carry
 
-    def second_half(step, carry):
-        attend((batch(step, used), (1,)))
-        return carry
-
-    lax.fori_loop(0, LAG, first_half, 0)
-    lax.fori_loop(LAG, steps, both_halves, 0)
+    lax.fori_loop(0, steps, both_halves, 0)
 
     def swap(turn, way):
         return pltpu.make_async_remote_copy(
@@ -497,14 +503,11 @@
                 summed = summed + last_in[turn, way, side].astype(jnp.float32)
             out[turn * TURN : (turn + 1) * TURN, side * HALF : (side + 1) * HALF] = summed.astype(jnp.bfloat16)
 
-    middle = steps - LAG + 1
     close(0)
-    lax.fori_loop(steps - LAG, middle, second_half, 0)
+    close(1)
     deal(0)
-    lax.fori_loop(middle, steps, second_half, 0)
-    close(1)
+    deal(1)
     reorder(0)
-    deal(1)
     loads[6].wait()
     collect(0)
     project(0)

time: 93.1 us -> 88.8 us (0.954)
  Pallas kernels: 91.1 us -> 86.8 us
    pallas_call x1, Pallas kernels: 91.1 us -> 86.8 us  [local(): pl.pallas_call(kernel, out_shape=jax.ShapeDtypeStruct((ROWS // HEADS, WID...]
where the time goes in v6:
time: 88.8 us; the launch traced here: 88.7 us
  Pallas kernels  86.8 us (98%)
  local copies, waits for them, and re-layouts  1.87 us (2%)
    pallas_call x1, Pallas kernels, local(): pl.pallas_call(kernel, out_shape=jax.ShapeDtypeStruct((ROWS // HEADS, WID...  86.8 us
    unnamed x1, local copies, waits for them, and re-layouts  1.87 us

profile of v6, /device:TPU:1, one launch (start us, length us, event | category | flops | bytes accessed | tf_op | source)
XLA Modules:
  0.0 88.7 jit_solution(10655722604504626084)
XLA Ops:
  0.0 86.8 %attend_and_project.1 = bf16[64,4096]{1,0:T(8,128)(2,1)} custom-call(bf16[256,512]{1,0:T(8,128)(2,1)} %queries_hbm.1, bf16[256,128]{1,0:T(8,128)(2,1)} %keys_hbm.1, bf16[256,128]{1,0:T(8,128)(2,1)} %values_hbm.1, s32[2,128]{1,0:T(2,128)} %bitcast.4, s32[3,128]{1,0:T(4,128)} %bitcast.3, s32[1,128]{1,0:T(1,128)} %bitcast.5, bf16[512,4096]{1,0:T(8,128)(2,1)} %proj_hbm.1), custom_call_target="tpu_custom_call" | custom-call | flops 8589934592 | bytes 4194304 | tf_op jit(solution)/shard_map/attend_and_project/pallas_call | solution.py:543
  86.8 1.9 %copy.9 = bf16[64,4096]{1,0:T(8,128)(2,1)} copy(bf16[64,4096]{1,0:T(8,128)(2,1)} %attend_and_project.1) | data formatting | bytes 1048576

commit v7 on v6

--- a/solution.py
+++ b/solution.py
@@ -90,6 +90,7 @@
     held, scaled, total, top, recv_sem, send_sem,
     shuffle, swap_out, swap_in, spread_out, spread_in, back_in, mix, owned, swap_send, swap_recv, spread_send, spread_recv,
     part, first_in, last_in, sum_send, sum_recv,
+    tiles_out, tiles_in, tiles_back, tiles_send, tiles_recv,
 ):
     place = Place()
     me, core, other = place.ctx, place.core, 1 - place.core
@@ -418,11 +419,14 @@
         many = spread_out.at[way, turn, pl.ds(0, CHIPS - 1)]
         pltpu.make_async_copy(many, many, spread_send.at[way, turn]).wait()
 
-    def close(turn):
-        done = [
+    def attended(turn):
+        return [
             (total[rows, 0:HD] / total[rows, HD : 2 * HD]).astype(jnp.bfloat16)
             for rows in (rows_of(turn, head) for head in range(GROUP))
         ]
+
+    def close(turn):
+        done = attended(turn)
         for block in range(2):
             starts = [block * 2 * TURN + side * TURN for side in range(2)]
             planes = [done[head][start : start + TURN, :] for start in starts for head in range(GROUP)]
@@ -466,14 +470,16 @@
             device_id={"ctx": me, "head": place.plane(way)}, device_id_type=MESH,
         )
 
-    def project(turn):
+    def owned_rows(turn):
         swap(turn, 1).wait_recv()
         owned[turn, other] = swap_in[1, turn]
         lefts = []
         for block in range(2):
             sorted_rows = exact(shuffle[1], owned[turn, block]).astype(jnp.bfloat16)
             lefts.append(jnp.concatenate([sorted_rows[64 * head : 64 * (head + 1), :] for head in range(GROUP)], axis=1))
-        left = jnp.concatenate(lefts, axis=0)
+        return jnp.concatenate(lefts, axis=0)
+
+    def project(turn, left):
         for side in range(2):
             for at in range(2):
                 start = side * HALF + at * (HALF // 2)
@@ -501,23 +507,59 @@
             summed = part[turn, place.head, side].astype(jnp.float32)
             for way in range(2):
                 summed = summed + last_in[turn, way, side].astype(jnp.float32)
-            out[turn * TURN : (turn + 1) * TURN, side * HALF : (side + 1) * HALF] = summed.astype(jnp.bfloat16)
-
+            summed = summed.astype(jnp.bfloat16)
+            if turn == 0:
+                out[0:TURN, side * HALF : (side + 1) * HALF] = summed
+                continue
+            for at in range(HALF // HD):
+                tiles_out[0, side * (HALF // HD) + at] = summed[:, at * HD : (at + 1) * HD]
+
+    def tile_spread(way):
+        target = tiles_in.at[0] if way == 0 else tiles_back
+
+        def one(step, carry):
+            there = ctx_of((place.x + step // NZ) % NX, (place.z + step % NZ) % NZ, core)
+            pltpu.make_async_remote_copy(
+                src_ref=tiles_out.at[way, there // CORES], dst_ref=target.at[place.chip_here],
+                send_sem=tiles_send.at[way], recv_sem=tiles_recv.at[way],
+                device_id=place.device(there), device_id_type=MESH,
+            ).start()
+            return carry
+
+        lax.fori_loop(1, CHIPS, one, 0)
+        target[place.chip_here] = tiles_out[way, place.chip_here]
+
+    def tiles_wait(sem):
+        many = tiles_back.at[pl.ds(0, CHIPS - 1)]
+        pltpu.make_async_copy(many, many, sem).wait()
+
+    tile_swap = pltpu.make_async_remote_copy(
+        src_ref=tiles_in.at[0], dst_ref=tiles_in.at[1], send_sem=tiles_send.at[2], recv_sem=tiles_recv.at[2],
+        device_id=sibling, device_id_type=MESH,
+    )
+
+    def tiles_choose():
+        tile_swap.wait_recv()
+        for chip in range(CHIPS):
+            mine = (owner[...] == CORES * chip + core) & (lane % 2 == place.head // 2)
+            home = jnp.clip(jnp.sum(jnp.where(mine, lane, 0)) // 2, 0, CTX - 1)
+            tiles_out[1, chip] = tiles_in[(home + core) % 2, home // 2]
+
+    loads[6].wait()
+    project(1, jnp.concatenate(attended(1), axis=1))
     close(0)
-    close(1)
     deal(0)
-    deal(1)
+    relay(1)
     reorder(0)
-    loads[6].wait()
     collect(0)
-    project(0)
-    reorder(1)
+    finish(1)
+    tile_spread(0)
+    project(0, owned_rows(0))
     relay(0)
-    collect(1)
-    project(1)
-    relay(1)
-    finish(0)
-
+    tiles_wait(tiles_recv.at[0])
+    tile_swap.start()
+    tiles_choose()
+    tile_spread(1)
     for role in range(2):
 
         @pl.when(core == role)
@@ -526,12 +568,17 @@
                 for each in sends(role, index):
                     each.wait_send()
 
-    finish(1)
-
+    finish(0)
+    tiles_wait(tiles_recv.at[1])
+    for at in range(CHIPS):
+        out[TURN : 2 * TURN, at * HD : (at + 1) * HD] = tiles_back[at]
+
+    for way in range(2):
+        swap(0, way).wait_send()
+        spread_sent(0, way)
+        tiles_wait(tiles_send.at[way])
+    tile_swap.wait_send()
     for turn in range(2):
-        for way in range(2):
-            swap(turn, way).wait_send()
-            spread_sent(turn, way)
         for message in range(6):
             give(turn, message).wait_send()
 
@@ -576,6 +623,11 @@
             pltpu.VMEM((2, 2, 2, TURN, HALF), bf16),
             dma((2, 6)),
             dma((2, 6)),
+            pltpu.VMEM((2, CHIPS, TURN, HD), bf16),
+            pltpu.VMEM((2, CHIPS, TURN, HD), bf16),
+            pltpu.VMEM((CHIPS, TURN, HD), bf16),
+            dma((3,)),
+            dma((3,)),
         ],
         compiler_params=pltpu.CompilerParams(
             collective_id=0, has_side_effects=True, vmem_limit_bytes=60 << 20

time: 88.8 us -> 86.7 us (0.976)
  Pallas kernels: 86.8 us -> 84.8 us
    pallas_call x1, Pallas kernels: 86.8 us -> 84.8 us  [local(): pl.pallas_call(kernel, out_shape=jax.ShapeDtypeStruct((ROWS // HEADS, WID...]
where the time goes in v7:
time: 86.7 us; the launch traced here: 86.6 us
  Pallas kernels  84.8 us (98%)
  local copies, waits for them, and re-layouts  1.87 us (2%)
    pallas_call x1, Pallas kernels, local(): pl.pallas_call(kernel, out_shape=jax.ShapeDtypeStruct((ROWS // HEADS, WID...  84.8 us
    unnamed x1, local copies, waits for them, and re-layouts  1.87 us

profile of v7, /device:TPU:1, one launch (start us, length us, event | category | flops | bytes accessed | tf_op | source)
XLA Modules:
  0.0 86.6 jit_solution(13171411795854313956)
XLA Ops:
  0.0 84.8 %attend_and_project.1 = bf16[64,4096]{1,0:T(8,128)(2,1)} custom-call(bf16[256,512]{1,0:T(8,128)(2,1)} %queries_hbm.1, bf16[256,128]{1,0:T(8,128)(2,1)} %keys_hbm.1, bf16[256,128]{1,0:T(8,128)(2,1)} %values_hbm.1, s32[2,128]{1,0:T(2,128)} %bitcast.4, s32[3,128]{1,0:T(4,128)} %bitcast.3, s32[1,128]{1,0:T(1,128)} %bitcast.5, bf16[512,4096]{1,0:T(8,128)(2,1)} %proj_hbm.1), custom_call_target="tpu_custom_call" | custom-call | flops 8589934592 | bytes 4194304 | tf_op jit(solution)/shard_map/attend_and_project/pallas_call | solution.py:590
  84.8 1.9 %copy.9 = bf16[64,4096]{1,0:T(8,128)(2,1)} copy(bf16[64,4096]{1,0:T(8,128)(2,1)} %attend_and_project.1) | data formatting | bytes 1048576

commit v8 on v7

--- a/solution.py
+++ b/solution.py
@@ -538,11 +538,17 @@
         device_id=sibling, device_id_type=MESH,
     )
 
-    def tiles_choose():
-        tile_swap.wait_recv()
+    def tile_homes():
+        homes = []
         for chip in range(CHIPS):
             mine = (owner[...] == CORES * chip + core) & (lane % 2 == place.head // 2)
             home = jnp.clip(jnp.sum(jnp.where(mine, lane, 0)) // 2, 0, CTX - 1)
+            homes.append(home)
+        return homes
+
+    def tiles_choose(homes):
+        tile_swap.wait_recv()
+        for chip, home in enumerate(homes):
             tiles_out[1, chip] = tiles_in[(home + core) % 2, home // 2]
 
     loads[6].wait()
@@ -551,14 +557,15 @@
     deal(0)
     relay(1)
     reorder(0)
-    collect(0)
     finish(1)
     tile_spread(0)
+    collect(0)
     project(0, owned_rows(0))
     relay(0)
+    homes = tile_homes()
     tiles_wait(tiles_recv.at[0])
     tile_swap.start()
-    tiles_choose()
+    tiles_choose(homes)
     tile_spread(1)
     for role in range(2):
 

time: 86.7 us -> 86.3 us (level)
  no operation moved by 1% of the time
where the time goes in v8:
time: 86.3 us; the launch traced here: 86.2 us
  Pallas kernels  84.3 us (98%)
  local copies, waits for them, and re-layouts  1.87 us (2%)
    pallas_call x1, Pallas kernels, local(): pl.pallas_call(kernel, out_shape=jax.ShapeDtypeStruct((ROWS // HEADS, WID...  84.3 us
    unnamed x1, local copies, waits for them, and re-layouts  1.87 us

profile of v8, /device:TPU:1, one launch (start us, length us, event | category | flops | bytes accessed | tf_op | source)
XLA Modules:
  0.0 86.2 jit_solution(4040711069961623246)
XLA Ops:
  0.0 84.3 %attend_and_project.1 = bf16[64,4096]{1,0:T(8,128)(2,1)} custom-call(bf16[256,512]{1,0:T(8,128)(2,1)} %queries_hbm.1, bf16[256,128]{1,0:T(8,128)(2,1)} %keys_hbm.1, bf16[256,128]{1,0:T(8,128)(2,1)} %values_hbm.1, s32[2,128]{1,0:T(2,128)} %bitcast.4, s32[3,128]{1,0:T(4,128)} %bitcast.3, s32[1,128]{1,0:T(1,128)} %bitcast.5, bf16[512,4096]{1,0:T(8,128)(2,1)} %proj_hbm.1), custom_call_target="tpu_custom_call" | custom-call | flops 8589934592 | bytes 4194304 | tf_op jit(solution)/shard_map/attend_and_project/pallas_call | solution.py:597
  84.3 1.9 %copy.9 = bf16[64,4096]{1,0:T(8,128)(2,1)} copy(bf16[64,4096]{1,0:T(8,128)(2,1)} %attend_and_project.1) | data formatting | bytes 1048576
